TPU v7x, 128 devices: a whole 4x4x4 slice. The times are simulated.
128 devices in a mesh: row: 8 (over z, core), col: 16 (over y, x).
Axes of the slice: x: 4, y: 4, z: 4, core: 2. Of those that a mesh axis runs over, the one named last changes fastest.
Arguments:
- a_tiles: float32 [2048, 128, 128], P(('row', 'col')), may hold values from -6 to 6
- a_index: int32 [2048], P(('row', 'col')), may hold values from 0 to 4095, as said below
- d_values: float32 [4096, 8192], P('row', 'col'), may hold values from -0.1875 to 0.1875
- d_mask: int32 [32, 64], P('row', 'col'), may hold values 0 or 1
Outputs:
- contracted: float32 [16384, 8192], P('row', 'col')
Inputs may be any that keep to these rules, and one draw needn't show every extreme that they name: `a_index`: the stored positions are distinct. Device s (in the order row then col) holds entries s * 16 to s * 16 + 15, and each has block row between 16 * r and 16 * r + 15, r being that device's row index. With the device at row r and column c owning block rows 16 * r to 16 * r + 15 and block columns 2 * c to 2 * c + 1, at most 2 blocks of one device are owned by one device, reached in every draw; in every row of devices one device owns 16 * 2 stored blocks and another none.
All inputs are finite; a program needn't handle non-finite values. No bound on the sum of `d_mask` on one device may be relied on, other than what follows from the above.
Results may differ from a plain program's by a relative error of at most 0.00007.
Values sent between devices are 32-bit elements; how exact they have to be, the bound alone decides.
No kernel may reach another device: no remote copies, remote signals or barrier semaphores. Data moves between devices by JAX's collectives and lax.ppermute only.
A program may use at most 320 MiB of HBM per device.

v0:
```python
import jax
import jax.numpy as jnp
from jax import lax
from jax.sharding import PartitionSpec as P

MBL = 16
KBL = 2


def body(a_tiles, a_index, d_values, d_mask):
    tile_size = a_tiles.shape[1]
    across = lax.axis_size("col")
    kb_count = KBL * across
    my_row = lax.axis_index("row")
    kb_local = d_values.shape[0] // tile_size
    col_width = d_values.shape[1]
    masked = (
        d_values.reshape(kb_local, tile_size, d_mask.shape[1], tile_size)
        * d_mask.astype(jnp.float32)[:, None, :, None]
    ).reshape(kb_local * tile_size, col_width)
    density = lax.all_gather(masked, "row", axis=0, tiled=True)
    cell_count = MBL * KBL
    stored = a_tiles.shape[0]
    capacity = -(-cell_count // across)
    block_row = a_index // kb_count
    block_col = a_index % kb_count
    owner_col = block_col // KBL
    local_place = (block_row - my_row * MBL) * KBL + block_col % KBL
    same_owner = owner_col[:, None] == owner_col[None, :]
    earlier = jnp.arange(stored)[None, :] < jnp.arange(stored)[:, None]
    rank_within = jnp.sum((same_owner & earlier).astype(jnp.int32), axis=1)
    slot_index = owner_col * capacity + rank_within
    placing = slot_index[None, :] == jnp.arange(across * capacity, dtype=jnp.int32)[:, None]
    outgoing = jnp.einsum(
        "qs,sij->qij", placing.astype(jnp.float32), a_tiles, precision=lax.Precision.HIGHEST
    )
    out_place = jnp.max(jnp.where(placing, local_place[None, :] + 1, 0), axis=1) - 1
    incoming, in_place = (
        lax.all_to_all(outgoing, "col", split_axis=0, concat_axis=0, tiled=True),
        lax.all_to_all(out_place, "col", split_axis=0, concat_axis=0, tiled=True),
    )
    settle = (in_place[None, :] == jnp.arange(cell_count, dtype=jnp.int32)[:, None]).astype(
        jnp.float32
    )
    blocks = jnp.einsum("pq,qij->pij", settle, incoming, precision=lax.Precision.HIGHEST)
    panel = (
        blocks.reshape(MBL, KBL, tile_size, tile_size)
        .transpose(0, 2, 1, 3)
        .reshape(MBL * tile_size, KBL * tile_size)
    )
    return jnp.dot(
        lax.all_gather(panel, "col", axis=1, tiled=True),
        density,
        precision=lax.Precision.HIGHEST,
        preferred_element_type=jnp.float32,
    )


def solution(mesh):
    in_specs = (P(("row", "col"), None, None), P(("row", "col")), P("row", "col"), P("row", "col"))
    out_specs = P("row", "col")
    return jax.shard_map(body, mesh=mesh, in_specs=in_specs, out_specs=out_specs, check_vma=False)
```

profile of v0, /device:TPU:0, one launch (start us, length us, event | category | flops | bytes accessed | tf_op | source)
XLA Modules:
  0.0 329.6 jit_solution(13179287584074608958)
XLA Ops:
  6.5 0.0 copy-start
  6.5 0.0 all-gather.5.cloned.1.call-start
  6.5 0.8 convert_element_type.9
  7.3 0.2 mul.23
  7.5 0.0 copy-start.1
  7.5 2.4 bitcast_multiply_fusion
  9.9 0.0 all-gather.5.cloned.1.call-update
  10.0 0.0 copy-done.1
  10.0 0.2 convert_reduce_fusion
  10.2 0.1 select_reduce_fusion
  10.3 0.7 sub.24
  11.0 7.1 %all-to-all-start = ((s32[16,2,1]{1,2,0:T(1,128)}), s32[16,2,1]{1,2,0:T(1,128)S(1)}, u32[]{:S(2)}, u32[]{:S(2)}) async-start(s32[16,2,1]{1,2,0:T(1,128)} %bitcast), calls=%async_computation | async-start | bytes 16384 | tf_op jit(solution)/shard_map/all_to_all | solution.py:40
  18.1 0.0 copy-done
  18.1 1.6 fusion.2
  19.7 2.5 copy.13
  22.2 3.4 %all-to-all-done = s32[16,2,1]{1,2,0:T(1,128)S(1)} async-done(((s32[16,2,1]{1,2,0:T(1,128)}), s32[16,2,1]{1,2,0:T(1,128)S(1)}, u32[]{:S(2)}, u32[]{:S(2)}) %all-to-all-start) | async-done | bytes 160 | tf_op jit(solution)/shard_map/all_to_all | solution.py:40
  25.7 3.8 %all-to-all-start.1 = ((f32[32,128,128]{2,1,0:T(8,128)}), f32[32,128,128]{2,1,0:T(8,128)S(1)}, u32[]{:S(2)}, u32[]{:S(2)}) async-start(f32[32,128,128]{2,1,0:T(8,128)} %copy.13), calls=%async_computation.1 | async-start | bytes 4194304 | tf_op jit(solution)/shard_map/all_to_all | solution.py:39
  29.5 0.0 all-gather.3.cloned.1.call-start
  29.5 0.5 broadcast.76
  30.0 0.6 reduce.3
  30.7 0.1 eq.50
  30.8 29.0 %all-to-all-done.1 = f32[32,128,128]{2,1,0:T(8,128)S(1)} async-done(((f32[32,128,128]{2,1,0:T(8,128)}), f32[32,128,128]{2,1,0:T(8,128)S(1)}, u32[]{:S(2)}, u32[]{:S(2)}) %all-to-all-start.1) | async-done | bytes 2097184 | tf_op jit(solution)/shard_map/all_to_all | solution.py:39
  59.8 3.7 %fusion = f32[32,128,128]{2,0,1:T(8,128)} fusion(f32[32,128,128]{2,1,0:T(8,128)S(1)} %all-to-all-done.1, s32[32]{0:T(128)S(1)} %eq.50), kind=kOutput, calls=%fused_computation.1 | convolution fusion | flops 201327616 | bytes 4194432 | tf_op jit(solution)/shard_map/pq,qij->pij/dot_general | solution.py:45
  63.5 2.3 copy.15
  65.8 2.2 copy.24
  68.0 0.0 all-gather.3.cloned.1.call-update
  68.0 0.0 all-gather.5.cloned.1.call-done
  68.0 195.6 %all-gather.3.cloned.1.call-done = f32[2048,4096]{0,1:T(8,128)} async-done(((f32[2048,256]{0,1:T(8,128)}), f32[2048,4096]{0,1:T(8,128)}) %all-gather.3.cloned.1.call-update) | async-done | bytes 33554448 | tf_op jit(solution)/shard_map/all_gather | solution.py:52
  263.6 59.2 %fusion.13 = f32[2048,512]{1,0:T(8,128)} fusion(f32[2048,4096]{0,1:T(8,128)} %all-gather.3.cloned.1.call-done, f32[4096,512]{1,0:T(8,128)} %all-gather.5.cloned.1.call-done), kind=kOutput, calls=%fused_computation.30 | convolution fusion | flops 51539607552 | bytes 46137344 | tf_op jit(solution)/shard_map/dot_general | solution.py:51
  (4 shorter events, 0.0 us)
Async XLA Ops:
  6.5 11.6 %copy-start = (f32[16,128,128]{2,1,0:T(8,128)S(1)}, f32[16,128,128]{2,1,0:T(8,128)}, u32[]{:S(2)}) copy-start(f32[16,128,128]{2,1,0:T(8,128)} %param.4) | copy-start | bytes 3145732
  6.5 61.5 %all-gather.5.cloned.1.call-start = ((), (), s32[]{:S(2)}) async-start(), calls=%async_computation.3 | async-start | bytes 9437184 | tf_op jit(solution)/shard_map/all_gather | solution.py:21
  7.5 2.4 copy-start.1
  11.0 14.7 %all-to-all-start = ((s32[16,2,1]{1,2,0:T(1,128)}), s32[16,2,1]{1,2,0:T(1,128)S(1)}, u32[]{:S(2)}, u32[]{:S(2)}) async-start(s32[16,2,1]{1,2,0:T(1,128)} %bitcast), calls=%async_computation | async-start | bytes 16384 | tf_op jit(solution)/shard_map/all_to_all | solution.py:40
  25.7 34.1 %all-to-all-start.1 = ((f32[32,128,128]{2,1,0:T(8,128)}), f32[32,128,128]{2,1,0:T(8,128)S(1)}, u32[]{:S(2)}, u32[]{:S(2)}) async-start(f32[32,128,128]{2,1,0:T(8,128)} %copy.13), calls=%async_computation.1 | async-start | bytes 4194304 | tf_op jit(solution)/shard_map/all_to_all | solution.py:39
  29.5 234.1 %all-gather.3.cloned.1.call-start = ((), (), s32[]{:S(2)}) async-start(), calls=%async_computation.2 | async-start | bytes 35651584 | tf_op jit(solution)/shard_map/all_gather | solution.py:52
Sparse Core Ops, SparseCore 0:
  10.1 52.3 all-gather.4
  68.1 195.4 all-gather.2
where the time goes:
time: 331 us; the launch traced here: 330 us
  waiting for transfers between devices  228 us (69%)
  matrix products  64.5 us (19%)
  between operations  13.5 us (4%)
  starting transfers between devices  10.9 us (3%)
  local copies, waits for them, and re-layouts  8.52 us (3%)
  other arithmetic  4.13 us (1%)
    all_gather x1, waiting for transfers between devices, body(): lax.all_gather(panel, 'col', axis=1, tiled=True)  196 us
    dot_general x1, matrix products, body(): jnp.dot(lax.all_gather(panel, 'col', axis=1, tiled=True), density, precis...  59.2 us
    all_to_all x1, waiting for transfers between devices, body(): lax.all_to_all(outgoing, 'col', split_axis=0, concat_axis=0, tiled=True)  29 us
    all_to_all x1, starting transfers between devices, body(): lax.all_to_all(out_place, 'col', split_axis=0, concat_axis=0, tiled=True)  7.12 us
  transfers between devices with their start and end apart: 4, of which 3 were waited for; matrix products, arithmetic and copies ran while one was open for 4% of the time, Pallas kernels for 0%

commit v1 on v0

v1 whole, which is shorter than its diff:
```python
import functools

import jax
import jax.numpy as jnp
from jax import lax
from jax.experimental import pallas as pl
from jax.experimental.pallas import tpu as pltpu
from jax.sharding import Mesh, PartitionSpec as P

MBL = 16
KB = 32
NY = 4
NX = 4
HALF = 8
MARK = 8
MIB = 2**20


def ring(v, axis, n):
    perm = []
    for q, step in ((0, 1), (1, -1)):
        for i in range(n):
            at = [(j * 2 + q if axis == "z" else q * n + j) for j in (i, (i + step) % n)]
            perm.append(tuple(at))
    return lax.ppermute(v, ("z", "core") if axis == "z" else ("core", axis), perm)


def step_both(pair):
    return lax.optimization_barrier((ring(pair[0], "x", NX), ring(pair[1], "y", NY)))


def mask_kernel(mask_ref, d_ref, out_ref):
    size = out_ref.shape[0] // mask_ref.shape[0]
    for i in range(mask_ref.shape[0]):
        for j in range(mask_ref.shape[1]):
            block = slice(i * size, (i + 1) * size), slice(j * size, (j + 1) * size)
            out_ref[block] = d_ref[block] * mask_ref[i, j].astype(jnp.float32)


def mask_blocks(mask, d):
    return pl.pallas_call(
        mask_kernel,
        in_specs=[pl.BlockSpec(memory_space=pltpu.SMEM), pl.BlockSpec(memory_space=pltpu.VMEM)],
        out_specs=pl.BlockSpec(memory_space=pltpu.VMEM),
        out_shape=pltpu.VMEM(d.shape, jnp.float32),
        compiler_params=pltpu.CompilerParams(vmem_limit_bytes=8 * MIB),
        cost_estimate=pl.CostEstimate(flops=d.size, bytes_accessed=8 * d.size, transcendentals=0),
    )(mask, d)


def after(pair, others):
    return lax.optimization_barrier((*pair, *others))[: len(pair)]


def split_kernel(d_ref, hi_ref, lo_ref):
    d = d_ref[...]
    hi = d.astype(jnp.bfloat16)
    hi_ref[...] = hi
    lo_ref[...] = (d - hi.astype(jnp.float32)).astype(jnp.bfloat16)


def split(d):
    rows, width = d.shape
    block = 512
    spec = pl.BlockSpec((block, width), lambda i: (i, 0))
    return pl.pallas_call(
        split_kernel,
        grid=(rows // block,),
        in_specs=[spec],
        out_specs=[spec, spec],
        out_shape=[pltpu.VMEM(d.shape, jnp.bfloat16)] * 2,
        compiler_params=pltpu.CompilerParams(vmem_limit_bytes=8 * MIB),
        cost_estimate=pl.CostEstimate(
            flops=4 * rows * width, bytes_accessed=8 * rows * width, transcendentals=0
        ),
    )(d)


def add_kernel(marks, first, size, *refs):
    n = len(marks)
    places, sem = refs[-1 - n : -1], refs[-1]
    out = refs[-2 - n]
    if first:
        hi_ref, lo_ref, *tiles = refs[: -2 - n]
    else:
        acc, hi_ref, lo_ref, *tiles = refs[: -2 - n]
    copies = [
        pltpu.make_async_copy(t.at[pl.ds(len(m) * size, p.shape[0]), :], p, sem.at[i])
        for i, (t, m, p) in enumerate(zip(tiles, marks, places))
    ]
    for c in copies:
        c.start()
    out[...] = jnp.zeros_like(out) if first else acc[...]
    for c in copies:
        c.wait()
    todo = [(i, m) for i, mark in enumerate(marks) for m in range(len(mark))]
    group = 16 if len(todo) % 16 == 0 else 12
    for at in range(0, len(todo), group):
        products = []
        for i, m in todo[at : at + group]:
            place = places[i][marks[i][m]].astype(jnp.int32)
            k = pl.multiple_of((place & (KB - 1)) * size, size)
            t = tiles[i][m * size : (m + 1) * size, :]
            hi = t.astype(jnp.bfloat16)
            lo = (t - hi.astype(jnp.float32)).astype(jnp.bfloat16)
            dhi = hi_ref[pl.ds(k, size), :]
            dlo = lo_ref[pl.ds(k, size), :]
            product = jnp.dot(
                jnp.concatenate([hi, lo], axis=1),
                jnp.concatenate([dhi, dhi], axis=0),
                preferred_element_type=jnp.float32,
            ) + jnp.dot(hi, dlo, preferred_element_type=jnp.float32)
            products.append(((place // KB) & (MBL - 1), product))
        for r, product in products:
            out[pl.ds(pl.multiple_of(r * size, size), size), :] += product


def add_products(acc, hi, lo, tiles, marks, last=False):
    size = tiles[0].shape[1]
    depth, width = hi.shape
    first = acc is None
    vmem = pl.BlockSpec(memory_space=pltpu.VMEM)
    operands = ([] if first else [acc]) + [hi, lo, *tiles]
    total = sum(len(m) for m in marks)
    shape = (MBL * size, width)
    return pl.pallas_call(
        functools.partial(add_kernel, marks, first, size),
        in_specs=[vmem] * len(operands),
        out_specs=vmem,
        out_shape=jax.ShapeDtypeStruct(shape, jnp.float32) if last else pltpu.VMEM(shape, jnp.float32),
        input_output_aliases={} if first or last else {0: 0},
        scratch_shapes=[
            pltpu.SMEM((t.shape[0] - len(m) * size, size), jnp.float32) for t, m in zip(tiles, marks)
        ]
        + [pltpu.SemaphoreType.DMA((len(tiles),))],
        compiler_params=pltpu.CompilerParams(vmem_limit_bytes=24 * MIB),
        cost_estimate=pl.CostEstimate(
            flops=total * size * size * width * 12,
            bytes_accessed=total * size * size * 4,
            transcendentals=0,
        ),
    )(*operands)


def body(a_tiles, a_index, d_values, d_mask):
    stored, size = a_tiles.shape[0], a_tiles.shape[1]
    few = HALF // 2
    data = HALF * size
    density = lax.all_gather(mask_blocks(d_mask, d_values), ("z", "core"), axis=0, tiled=True)

    flat = a_tiles.reshape(stored * size, size)
    position = a_index.astype(jnp.float32)

    def payload(n):
        lanes = jnp.pad(position[n * HALF : (n + 1) * HALF], (0, size - HALF))
        return jnp.concatenate([flat[n * data : (n + 1) * data], jnp.broadcast_to(lanes, (MARK, size))])

    whole = [(0, j) for j in range(HALF)]

    def early(u, v):
        return jnp.concatenate([u[:data], v[: data // 2], u[data:], v[data:]])

    early_marks = whole + [(MARK, j) for j in range(few)]

    def late(u, v):
        return jnp.concatenate([u[data // 2 : data], v[:data], u[data:], v[data:]])

    late_marks = [(0, j) for j in range(few, HALF)] + [(MARK, j) for j in range(HALF)]

    a, b = payload(0), payload(1)
    p, q = [(a, b)], [(b, a)]
    for n in range(3):
        p.append(step_both(after(p[n], q[n - 1]) if n else p[n]))
        q.append(step_both(after(q[n], p[n]) if n else q[n]))
    (a1, b1), (a2, b2), (a3, b3) = p[1:]
    p4 = step_both(after((early(b1, b2), early(a1, a2)), q[2]))
    q4 = step_both(after((late(b2, b3), late(a2, a3)), q[3]))
    *p4, density = lax.optimization_barrier((*p4, density))
    *q4, density = lax.optimization_barrier((*q4, density))
    hi, lo = split(density)

    def add(acc, pairs, marks, **kw):
        tiles = [t for pair in pairs for t in pair]
        return add_products(acc, hi, lo, tiles, [m for m in marks for _ in range(2)], **kw)

    p5 = step_both(p4)
    q5 = step_both(q4)
    p6 = step_both(p5)
    q6 = step_both(q5)
    acc = add(None, [(a, b), p[1], q[1], p[2]], [whole] * 4)
    acc = add(acc, [q[2], p[3], q[3]], [whole] * 3)
    acc = add(acc, [p4, q4], [early_marks, late_marks])
    acc = add(acc, [p5, q5], [early_marks, late_marks])
    return add(acc, [p6, q6], [early_marks, late_marks], last=True)


def solution(mesh):
    grid = Mesh(mesh.devices.reshape(-1, 2, NY, NX), ("z", "core", "y", "x"))
    row, col = ("z", "core"), ("y", "x")
    in_specs = (P(row + col, None, None), P(row + col), P(row, col), P(row, col))
    return jax.shard_map(
        body, mesh=grid, in_specs=in_specs, out_specs=P(row, col), check_vma=False
    )
```

time: 331 us -> 137 us (0.41)
  waiting for transfers between devices: 228 us -> 57.7 us
  matrix products: 64.5 us -> 0 us
  Pallas kernels: 0 us -> 29.8 us
  starting transfers between devices: 10.9 us -> 20.8 us
  local copies, waits for them, and re-layouts: 8.52 us -> 14.2 us
    all_gather x2 -> x1, waiting for transfers between devices: 196 us -> 0.01 us  [body(): lax.all_gather(mask_blocks(d_mask, d_values), ('z', 'core'), axis=0, tile...]
    dot_general x3 -> x0, matrix products: 64.5 us -> none  [the longest x1 59.2 us: body(): jnp.dot(lax.all_gather(panel, 'col', axis=1, tiled=True), density, precis...]
    ppermute x0 -> x24, waiting for transfers between devices: none -> 57.7 us  [ring(): lax.ppermute(v, ('z', 'core') if axis == 'z' else ('core', axis), perm)]
    all_to_all x2 -> x0, waiting for transfers between devices: 32.4 us -> none  [the longest x1 29 us: body(): lax.all_to_all(outgoing, 'col', split_axis=0, concat_axis=0, tiled=True)]
    pallas_call x0 -> x7, Pallas kernels: none -> 29.8 us  [the longest x5 26.9 us: add_products(): pl.pallas_call(functools.partial(add_kernel, marks, first, size), in_spec...]
    ppermute x0 -> x24, starting transfers between devices: none -> 20.8 us  [ring(): lax.ppermute(v, ('z', 'core') if axis == 'z' else ('core', axis), perm)]
    all_to_all x2 -> x0, starting transfers between devices: 10.9 us -> none  [the longest x1 7.12 us: body(): lax.all_to_all(out_place, 'col', split_axis=0, concat_axis=0, tiled=True)]
    unnamed x5 -> x54, local copies, waits for them, and re-layouts: 2.21 us -> 12.6 us
  transfers between devices with their start and end apart: 4 -> 25, of which waited for: 3 -> 19; matrix products, arithmetic and copies ran while one was open for 4% -> 2% of each run, Pallas kernels for 0% -> 15%
where the time goes in v1:
time: 137 us
  waiting for transfers between devices  57.7 us (42%)
  Pallas kernels  29.8 us (22%)
  starting transfers between devices  20.8 us (15%)
  local copies, waits for them, and re-layouts  14.2 us (10%)
  between operations  13.8 us (10%)
    ppermute x24, waiting for transfers between devices, ring(): lax.ppermute(v, ('z', 'core') if axis == 'z' else ('core', axis), perm)  57.7 us
    pallas_call x5, Pallas kernels, add_products(): pl.pallas_call(functools.partial(add_kernel, marks, first, size), in_spec...  26.9 us
    ppermute x24, starting transfers between devices, ring(): lax.ppermute(v, ('z', 'core') if axis == 'z' else ('core', axis), perm)  20.8 us
    unnamed x54, local copies, waits for them, and re-layouts  12.6 us
  transfers between devices with their start and end apart: 25, of which 19 were waited for; matrix products, arithmetic and copies ran while one was open for 2% of the time, Pallas kernels for 15%

profile of v1, /device:TPU:0, one launch (start us, length us, event | category | flops | bytes accessed | tf_op | source)
XLA Modules:
  0.0 137.2 jit_solution(16415793034442749030)
XLA Ops:
  6.5 1.2 copy-done.1
  7.8 0.7 copy-done.22
  8.4 1.6 %shard_map.46 = f32[512,512]{1,0:T(8,128)} custom-call(s32[4,4]{1,0:T(4,128)S(1)} %copy-done.22, f32[512,512]{1,0:T(8,128)S(1)} %copy-done.1), custom_call_target="tpu_custom_call" | custom-call | flops 262144 | bytes 2097152 | tf_op jit(solution)/shard_map/pallas_call | solution.py:41
  10.1 0.0 all-gather.2.cloned.1.call-update
  10.1 0.7 convert_element_type.6
  10.8 0.1 fusion.3
  10.9 1.3 fusion
  12.2 1.6 %collective-permute-start = (f32[1032,128]{1,0:T(8,128)S(1)}, f32[1032,128]{1,0:T(8,128)S(1)}, u32[]{:S(2)}, u32[]{:S(2)}) collective-permute-start(f32[1032,128]{1,0:T(8,128)S(1)} %pad_maximum_fusion.4.refs_2_), channel_id=1, source_target_pairs={{0,1},{1,2},{2,3},{3,0},{16,19},{17,16},{18,17},{19,18},{4,5},{5,6... | collective-permute-start | bytes 1585160 | tf_op jit(solution)/shard_map/ppermute | solution.py:25
  13.9 1.6 %collective-permute-start.1 = (f32[1032,128]{1,0:T(8,128)S(1)}, f32[1032,128]{1,0:T(8,128)S(1)}, u32[]{:S(2)}, u32[]{:S(2)}) collective-permute-start(f32[1032,128]{1,0:T(8,128)S(1)} %pad_maximum_fusion.5.refs_3_), channel_id=1, source_target_pairs={{0,4},{4,8},{8,12},{12,0},{16,28},{20,16},{24,20},{28,24},{1,5},{5... | collective-permute-start | bytes 1585160 | tf_op jit(solution)/shard_map/ppermute | solution.py:25
  15.6 1.6 %collective-permute-start.5 = (f32[1032,128]{1,0:T(8,128)S(1)}, f32[1032,128]{1,0:T(8,128)S(1)}, u32[]{:S(2)}, u32[]{:S(2)}) collective-permute-start(f32[1032,128]{1,0:T(8,128)S(1)} %pad_maximum_fusion.4.refs_2_), channel_id=1, source_target_pairs={{0,4},{4,8},{8,12},{12,0},{16,28},{20,16},{24,20},{28,24},{1,5},{5... | collective-permute-start | bytes 1585160 | tf_op jit(solution)/shard_map/ppermute | solution.py:25
  17.1 1.5 %collective-permute-start.4 = (f32[1032,128]{1,0:T(8,128)S(1)}, f32[1032,128]{1,0:T(8,128)S(1)}, u32[]{:S(2)}, u32[]{:S(2)}) collective-permute-start(f32[1032,128]{1,0:T(8,128)S(1)} %pad_maximum_fusion.5.refs_3_), channel_id=1, source_target_pairs={{0,1},{1,2},{2,3},{3,0},{16,19},{17,16},{18,17},{19,18},{4,5},{5,6... | collective-permute-start | bytes 1585160 | tf_op jit(solution)/shard_map/ppermute | solution.py:25
  18.6 0.8 copy-done.4
  19.4 3.3 %collective-permute-done.refs_4_ = f32[1032,128]{1,0:T(8,128)S(1)} collective-permute-done((f32[1032,128]{1,0:T(8,128)S(1)}, f32[1032,128]{1,0:T(8,128)S(1)}, u32[]{:S(2)}, u32[]{:S(2)}) %collective-permute-start) | collective-permute-done | bytes 528416 | tf_op jit(solution)/shard_map/ppermute | solution.py:25
  22.7 1.7 %collective-permute-done.1.refs_5_ = f32[1032,128]{1,0:T(8,128)S(1)} collective-permute-done((f32[1032,128]{1,0:T(8,128)S(1)}, f32[1032,128]{1,0:T(8,128)S(1)}, u32[]{:S(2)}, u32[]{:S(2)}) %collective-permute-start.1) | collective-permute-done | bytes 528416 | tf_op jit(solution)/shard_map/ppermute | solution.py:25
  24.4 1.5 %collective-permute-start.2 = (f32[1032,128]{1,0:T(8,128)S(1)}, f32[1032,128]{1,0:T(8,128)S(1)}, u32[]{:S(2)}, u32[]{:S(2)}) collective-permute-start(f32[1032,128]{1,0:T(8,128)S(1)} %collective-permute-done.refs_4_), channel_id=1, source_target_pairs={{0,1},{1,2},{2,3},{3,0},{16,19},{17,16},{18,17},{19,18},{4,5},{5,6... | collective-permute-start | bytes 1585160 | tf_op jit(solution)/shard_map/ppermute | solution.py:25
  25.9 0.4 collective-permute-start.3
  26.3 3.8 %collective-permute-done.5.refs_7_ = f32[1032,128]{1,0:T(8,128)S(1)} collective-permute-done((f32[1032,128]{1,0:T(8,128)S(1)}, f32[1032,128]{1,0:T(8,128)S(1)}, u32[]{:S(2)}, u32[]{:S(2)}) %collective-permute-start.5) | collective-permute-done | bytes 528416 | tf_op jit(solution)/shard_map/ppermute | solution.py:25
  30.1 1.5 %collective-permute-start.8 = (f32[1032,128]{1,0:T(8,128)S(1)}, f32[1032,128]{1,0:T(8,128)S(1)}, u32[]{:S(2)}, u32[]{:S(2)}) collective-permute-start(f32[1032,128]{1,0:T(8,128)S(1)} %collective-permute-done.4.refs_6_), channel_id=1, source_target_pairs={{0,1},{1,2},{2,3},{3,0},{16,19},{17,16},{18,17},{19,18},{4,5},{5,6... | collective-permute-start | bytes 1585160 | tf_op jit(solution)/shard_map/ppermute | solution.py:25
  31.6 0.8 copy-done.25
  32.4 0.4 collective-permute-start.9
  32.8 0.8 copy-done.23
  33.6 1.3 collective-permute-done.2.refs_8_
  34.9 1.5 %collective-permute-done.3.refs_9_ = f32[1032,128]{1,0:T(8,128)S(1)} collective-permute-done((f32[1032,128]{1,0:T(8,128)S(1)}, f32[1032,128]{1,0:T(8,128)S(1)}, u32[]{:S(2)}, u32[]{:S(2)}) %collective-permute-start.3) | collective-permute-done | bytes 528416 | tf_op jit(solution)/shard_map/ppermute | solution.py:25
  36.4 1.2 collective-permute-start.6
  37.6 0.1 collective-permute-start.7
  37.6 2.9 %collective-permute-done.8.refs_3_ = f32[1032,128]{1,0:T(8,128)S(1)} collective-permute-done((f32[1032,128]{1,0:T(8,128)S(1)}, f32[1032,128]{1,0:T(8,128)S(1)}, u32[]{:S(2)}, u32[]{:S(2)}) %collective-permute-start.8) | collective-permute-done | bytes 528416 | tf_op jit(solution)/shard_map/ppermute | solution.py:25
  40.5 2.3 %collective-permute-done.9.refs_4_ = f32[1032,128]{1,0:T(8,128)S(1)} collective-permute-done((f32[1032,128]{1,0:T(8,128)S(1)}, f32[1032,128]{1,0:T(8,128)S(1)}, u32[]{:S(2)}, u32[]{:S(2)}) %collective-permute-start.9) | collective-permute-done | bytes 528416 | tf_op jit(solution)/shard_map/ppermute | solution.py:25
  42.8 1.2 collective-permute-start.10
  44.0 0.8 copy-done.14
  44.8 0.8 copy-done.16
  45.7 0.8 copy-done.6
  46.5 0.1 fusion.1
  46.6 0.8 copy-done.12
  47.4 1.0 collective-permute-done.7.refs_6_
  48.6 4.7 %collective-permute-done.10.refs_7_ = f32[1032,128]{1,0:T(8,128)S(1)} collective-permute-done((f32[1032,128]{1,0:T(8,128)S(1)}, f32[1032,128]{1,0:T(8,128)S(1)}, u32[]{:S(2)}, u32[]{:S(2)}) %collective-permute-start.10) | collective-permute-done | bytes 528416 | tf_op jit(solution)/shard_map/ppermute | solution.py:25
  53.3 0.8 copy-done.18
  54.1 1.2 collective-permute-done.11.refs_8_
  55.3 0.8 copy-done.20
  56.1 0.1 pad_maximum_fusion.3
  56.2 0.1 pad_maximum_fusion.2
  56.3 0.5 collective-permute-start.12
  56.8 1.6 %collective-permute-start.14 = (f32[1552,128]{1,0:T(8,128)S(1)}, f32[1552,128]{1,0:T(8,128)S(1)}, u32[]{:S(2)}, u32[]{:S(2)}) collective-permute-start(f32[1552,128]{1,0:T(8,128)S(1)} %get-tuple-element.73), channel_id=1, source_target_pairs={{0,1},{1,2},{2,3},{3,0},{16,19},{17,16},{18,17},{19,18},{4,5},{5,6... | collective-permute-start | bytes 2383880 | tf_op jit(solution)/shard_map/ppermute | solution.py:25
  58.3 0.1 collective-permute-start.15
  58.5 11.2 %collective-permute-done.12.refs_5_ = f32[1552,128]{1,0:T(8,128)S(1)} collective-permute-done((f32[1552,128]{1,0:T(8,128)S(1)}, f32[1552,128]{1,0:T(8,128)S(1)}, u32[]{:S(2)}, u32[]{:S(2)}) %collective-permute-start.12) | collective-permute-done | bytes 794656 | tf_op jit(solution)/shard_map/ppermute | solution.py:25
  69.7 0.4 collective-permute-done.13.refs_6_
  70.0 8.1 %collective-permute-done.14.refs_3_ = f32[1552,128]{1,0:T(8,128)S(1)} collective-permute-done((f32[1552,128]{1,0:T(8,128)S(1)}, f32[1552,128]{1,0:T(8,128)S(1)}, u32[]{:S(2)}, u32[]{:S(2)}) %collective-permute-start.14) | collective-permute-done | bytes 794656 | tf_op jit(solution)/shard_map/ppermute | solution.py:25
  78.2 0.5 collective-permute-done.15.refs_4_
  78.7 3.4 %copy-done = f32[4096,512]{1,0:T(8,128)S(1)} copy-done((f32[4096,512]{1,0:T(8,128)S(1)}, f32[4096,512]{1,0:T(8,128)}, u32[]{:S(2)}) %copy-start) | copy-done | bytes 8388632
  82.1 1.2 shard_map.47
  83.3 1.6 %collective-permute-start.18 = (f32[1552,128]{1,0:T(8,128)S(1)}, f32[1552,128]{1,0:T(8,128)S(1)}, u32[]{:S(2)}, u32[]{:S(2)}) collective-permute-start(f32[1552,128]{1,0:T(8,128)S(1)} %collective-permute-done.12.refs_5_), channel_id=1, source_target_pairs={{0,1},{1,2},{2,3},{3,0},{16,19},{17,16},{18,17},{19,18},{4,5},{5,6... | collective-permute-start | bytes 2383880 | tf_op jit(solution)/shard_map/ppermute | solution.py:25
  85.0 1.5 %collective-permute-start.16 = (f32[1552,128]{1,0:T(8,128)S(1)}, f32[1552,128]{1,0:T(8,128)S(1)}, u32[]{:S(2)}, u32[]{:S(2)}) collective-permute-start(f32[1552,128]{1,0:T(8,128)S(1)} %collective-permute-done.14.refs_3_), channel_id=1, source_target_pairs={{0,1},{1,2},{2,3},{3,0},{16,19},{17,16},{18,17},{19,18},{4,5},{5,6... | collective-permute-start | bytes 2383880 | tf_op jit(solution)/shard_map/ppermute | solution.py:25
  86.5 0.0 collective-permute-start.17
  86.6 5.7 %shard_map.48.refs_0_ = f32[2048,512]{1,0:T(8,128)S(1)} custom-call(bf16[4096,512]{1,0:T(8,128)(2,1)S(1)} %get-tuple-element.79.refs_0_.refs_1_, bf16[4096,512]{1,0:T(8,128)(2,1)S(1)} %get-tuple-element.80.refs_1_.refs_2_, f32[1032,128]{1,0:T(8,128)S(1)} %copy-done.3, f32[1032,128]{1,0:T(8,128)S(1)} %copy-done.5, f32[1032,128]{1,0:T(8,128)S(1)} %copy-done.7, ...), custom_call_target="tpu_custom_call" | custom-call | flops 6442450944 | bytes 4194304 | tf_op jit(solution)/shard_map/pallas_call | solution.py:126
  92.3 4.5 %shard_map.49.refs_0_ = f32[2048,512]{1,0:T(8,128)S(1)} custom-call(f32[2048,512]{1,0:T(8,128)S(1)} %shard_map.48.refs_0_, bf16[4096,512]{1,0:T(8,128)(2,1)S(1)} %get-tuple-element.79.refs_0_.refs_1_, bf16[4096,512]{1,0:T(8,128)(2,1)S(1)} %get-tuple-element.80.refs_1_.refs_2_, f32[1032,128]{1,0:T(8,128)S(1)} %copy-done.15, ...), custom_call_target="tpu_custom_call", output_to_operand_aliasing={{}: (0, {})} | custom-call | flops 4831838208 | bytes 3145728 | tf_op jit(solution)/shard_map/pallas_call | solution.py:126
  96.8 1.5 %collective-permute-done.19.refs_6_ = f32[1552,128]{1,0:T(8,128)S(1)} collective-permute-done((f32[1552,128]{1,0:T(8,128)S(1)}, f32[1552,128]{1,0:T(8,128)S(1)}, u32[]{:S(2)}, u32[]{:S(2)}) %collective-permute-start.19) | collective-permute-done | bytes 794656 | tf_op jit(solution)/shard_map/ppermute | solution.py:25
  98.3 1.5 %collective-permute-start.22 = (f32[1552,128]{1,0:T(8,128)S(1)}, f32[1552,128]{1,0:T(8,128)S(1)}, u32[]{:S(2)}, u32[]{:S(2)}) collective-permute-start(f32[1552,128]{1,0:T(8,128)S(1)} %collective-permute-done.18.refs_5_), channel_id=1, source_target_pairs={{0,1},{1,2},{2,3},{3,0},{16,19},{17,16},{18,17},{19,18},{4,5},{5,6... | collective-permute-start | bytes 2383880 | tf_op jit(solution)/shard_map/ppermute | solution.py:25
  99.8 5.4 %collective-permute-done.16.refs_3_ = f32[1552,128]{1,0:T(8,128)S(1)} collective-permute-done((f32[1552,128]{1,0:T(8,128)S(1)}, f32[1552,128]{1,0:T(8,128)S(1)}, u32[]{:S(2)}, u32[]{:S(2)}) %collective-permute-start.16) | collective-permute-done | bytes 794656 | tf_op jit(solution)/shard_map/ppermute | solution.py:25
  105.2 1.6 %collective-permute-done.17.refs_4_ = f32[1552,128]{1,0:T(8,128)S(1)} collective-permute-done((f32[1552,128]{1,0:T(8,128)}, f32[1552,128]{1,0:T(8,128)S(1)}, u32[]{:S(2)}, u32[]{:S(2)}) %collective-permute-start.17) | collective-permute-done | bytes 794656 | tf_op jit(solution)/shard_map/ppermute | solution.py:25
  106.8 1.5 %collective-permute-start.20 = (f32[1552,128]{1,0:T(8,128)S(1)}, f32[1552,128]{1,0:T(8,128)S(1)}, u32[]{:S(2)}, u32[]{:S(2)}) collective-permute-start(f32[1552,128]{1,0:T(8,128)S(1)} %collective-permute-done.16.refs_3_), channel_id=1, source_target_pairs={{0,1},{1,2},{2,3},{3,0},{16,19},{17,16},{18,17},{19,18},{4,5},{5,6... | collective-permute-start | bytes 2383880 | tf_op jit(solution)/shard_map/ppermute | solution.py:25
  108.3 5.7 %shard_map.50.refs_0_ = f32[2048,512]{1,0:T(8,128)S(1)} custom-call(f32[2048,512]{1,0:T(8,128)S(1)} %shard_map.49.refs_0_, bf16[4096,512]{1,0:T(8,128)(2,1)S(1)} %get-tuple-element.79.refs_0_.refs_1_, bf16[4096,512]{1,0:T(8,128)(2,1)S(1)} %get-tuple-element.80.refs_1_.refs_2_, ...), custom_call_target="tpu_custom_call", output_to_operand_aliasing={{}: (0, {})} | custom-call | flops 4831838208 | bytes 3145728 | tf_op jit(solution)/shard_map/pallas_call | solution.py:126
  113.9 4.5 %shard_map.51.refs_0_ = f32[2048,512]{1,0:T(8,128)S(1)} custom-call(f32[2048,512]{1,0:T(8,128)S(1)} %shard_map.50.refs_0_, bf16[4096,512]{1,0:T(8,128)(2,1)S(1)} %get-tuple-element.79.refs_0_.refs_1_, bf16[4096,512]{1,0:T(8,128)(2,1)S(1)} %get-tuple-element.80.refs_1_.refs_2_, ...), custom_call_target="tpu_custom_call", output_to_operand_aliasing={{}: (0, {})} | custom-call | flops 4831838208 | bytes 3145728 | tf_op jit(solution)/shard_map/pallas_call | solution.py:126
  118.5 3.7 %collective-permute-done.20.refs_3_ = f32[1552,128]{1,0:T(8,128)S(1)} collective-permute-done((f32[1552,128]{1,0:T(8,128)S(1)}, f32[1552,128]{1,0:T(8,128)S(1)}, u32[]{:S(2)}, u32[]{:S(2)}) %collective-permute-start.20) | collective-permute-done | bytes 794656 | tf_op jit(solution)/shard_map/ppermute | solution.py:25
  122.2 1.6 %collective-permute-done.21.refs_4_ = f32[1552,128]{1,0:T(8,128)S(1)} collective-permute-done((f32[1552,128]{1,0:T(8,128)S(1)}, f32[1552,128]{1,0:T(8,128)S(1)}, u32[]{:S(2)}, u32[]{:S(2)}) %collective-permute-start.21) | collective-permute-done | bytes 794656 | tf_op jit(solution)/shard_map/ppermute | solution.py:25
  123.8 6.5 %shard_map.52 = f32[2048,512]{1,0:T(8,128)} custom-call(f32[2048,512]{1,0:T(8,128)S(1)} %shard_map.51.refs_0_, bf16[4096,512]{1,0:T(8,128)(2,1)S(1)} %get-tuple-element.79.refs_0_.refs_1_, bf16[4096,512]{1,0:T(8,128)(2,1)S(1)} %get-tuple-element.80.refs_1_.refs_2_, f32[1552,128]{1,0:T(8,128)S(1)} %collective-permute-done.20.refs_3_, ...), custom_call_target="tpu_custom_call" | custom-call | flops 4831838208 | bytes 3145728 | tf_op jit(solution)/shard_map/pallas_call | solution.py:126
  (70 shorter events, 0.4 us)
Async XLA Ops:
  6.5 72.1 %all-gather.2.cloned.1.call-start = ((), (), s32[]{:S(2)}) async-start(), calls=%async_computation | async-start | bytes 9437184 | tf_op jit(solution)/shard_map/all_gather | solution.py:149
  6.5 1.2 copy-start.1
  7.8 0.7 copy-start.22
  12.2 24.1 %copy-start.2 = (f32[1032,128]{1,0:T(8,128)}, f32[1032,128]{1,0:T(8,128)S(1)}, u32[]{:S(2)}) copy-start(f32[1032,128]{1,0:T(8,128)S(1)} %pad_maximum_fusion.4.refs_2_) | copy-start | bytes 1585156
  12.2 10.5 %collective-permute-start = (f32[1032,128]{1,0:T(8,128)S(1)}, f32[1032,128]{1,0:T(8,128)S(1)}, u32[]{:S(2)}, u32[]{:S(2)}) collective-permute-start(f32[1032,128]{1,0:T(8,128)S(1)} %pad_maximum_fusion.4.refs_2_), channel_id=1, source_target_pairs={{0,1},{1,2},{2,3},{3,0},{16,19},{17,16},{18,17},{19,18},{4,5},{5,6... | collective-permute-start | bytes 1585160 | tf_op jit(solution)/shard_map/ppermute | solution.py:25
  13.9 10.5 %collective-permute-start.1 = (f32[1032,128]{1,0:T(8,128)S(1)}, f32[1032,128]{1,0:T(8,128)S(1)}, u32[]{:S(2)}, u32[]{:S(2)}) collective-permute-start(f32[1032,128]{1,0:T(8,128)S(1)} %pad_maximum_fusion.5.refs_3_), channel_id=1, source_target_pairs={{0,4},{4,8},{8,12},{12,0},{16,28},{20,16},{24,20},{28,24},{1,5},{5... | collective-permute-start | bytes 1585160 | tf_op jit(solution)/shard_map/ppermute | solution.py:25
  15.6 14.5 %collective-permute-start.5 = (f32[1032,128]{1,0:T(8,128)S(1)}, f32[1032,128]{1,0:T(8,128)S(1)}, u32[]{:S(2)}, u32[]{:S(2)}) collective-permute-start(f32[1032,128]{1,0:T(8,128)S(1)} %pad_maximum_fusion.4.refs_2_), channel_id=1, source_target_pairs={{0,4},{4,8},{8,12},{12,0},{16,28},{20,16},{24,20},{28,24},{1,5},{5... | collective-permute-start | bytes 1585160 | tf_op jit(solution)/shard_map/ppermute | solution.py:25
  17.1 12.9 %collective-permute-start.4 = (f32[1032,128]{1,0:T(8,128)S(1)}, f32[1032,128]{1,0:T(8,128)S(1)}, u32[]{:S(2)}, u32[]{:S(2)}) collective-permute-start(f32[1032,128]{1,0:T(8,128)S(1)} %pad_maximum_fusion.5.refs_3_), channel_id=1, source_target_pairs={{0,1},{1,2},{2,3},{3,0},{16,19},{17,16},{18,17},{19,18},{4,5},{5,6... | collective-permute-start | bytes 1585160 | tf_op jit(solution)/shard_map/ppermute | solution.py:25
  18.6 0.8 copy-start.4
  24.4 24.1 %copy-start.8 = (f32[1032,128]{1,0:T(8,128)}, f32[1032,128]{1,0:T(8,128)S(1)}, u32[]{:S(2)}) copy-start(f32[1032,128]{1,0:T(8,128)S(1)} %collective-permute-done.1.refs_5_) | copy-start | bytes 1585156
  24.4 10.4 %collective-permute-start.2 = (f32[1032,128]{1,0:T(8,128)S(1)}, f32[1032,128]{1,0:T(8,128)S(1)}, u32[]{:S(2)}, u32[]{:S(2)}) collective-permute-start(f32[1032,128]{1,0:T(8,128)S(1)} %collective-permute-done.refs_4_), channel_id=1, source_target_pairs={{0,1},{1,2},{2,3},{3,0},{16,19},{17,16},{18,17},{19,18},{4,5},{5,6... | collective-permute-start | bytes 1585160 | tf_op jit(solution)/shard_map/ppermute | solution.py:25
  25.9 10.4 %collective-permute-start.3 = (f32[1032,128]{1,0:T(8,128)S(1)}, f32[1032,128]{1,0:T(8,128)S(1)}, u32[]{:S(2)}, u32[]{:S(2)}) collective-permute-start(f32[1032,128]{1,0:T(8,128)S(1)} %collective-permute-done.1.refs_5_), channel_id=1, source_target_pairs={{0,4},{4,8},{8,12},{12,0},{16,28},{20,16},{24,20},{28,24},{1,5},{5... | collective-permute-start | bytes 1585160 | tf_op jit(solution)/shard_map/ppermute | solution.py:25
  30.1 10.4 %collective-permute-start.8 = (f32[1032,128]{1,0:T(8,128)S(1)}, f32[1032,128]{1,0:T(8,128)S(1)}, u32[]{:S(2)}, u32[]{:S(2)}) collective-permute-start(f32[1032,128]{1,0:T(8,128)S(1)} %collective-permute-done.4.refs_6_), channel_id=1, source_target_pairs={{0,1},{1,2},{2,3},{3,0},{16,19},{17,16},{18,17},{19,18},{4,5},{5,6... | collective-permute-start | bytes 1585160 | tf_op jit(solution)/shard_map/ppermute | solution.py:25
  31.6 0.8 copy-start.25
  32.4 10.4 %collective-permute-start.9 = (f32[1032,128]{1,0:T(8,128)S(1)}, f32[1032,128]{1,0:T(8,128)S(1)}, u32[]{:S(2)}, u32[]{:S(2)}) collective-permute-start(f32[1032,128]{1,0:T(8,128)S(1)} %collective-permute-done.5.refs_7_), channel_id=1, source_target_pairs={{0,4},{4,8},{8,12},{12,0},{16,28},{20,16},{24,20},{28,24},{1,5},{5... | collective-permute-start | bytes 1585160 | tf_op jit(solution)/shard_map/ppermute | solution.py:25
  32.8 0.8 copy-start.23
  34.9 13.6 %copy-start.10 = (f32[1032,128]{1,0:T(8,128)}, f32[1032,128]{1,0:T(8,128)S(1)}, u32[]{:S(2)}) copy-start(f32[1032,128]{1,0:T(8,128)S(1)} %collective-permute-done.2.refs_8_) | copy-start | bytes 1585156
  36.4 11.1 %collective-permute-start.6 = (f32[1032,128]{1,0:T(8,128)S(1)}, f32[1032,128]{1,0:T(8,128)S(1)}, u32[]{:S(2)}, u32[]{:S(2)}) collective-permute-start(f32[1032,128]{1,0:T(8,128)S(1)} %collective-permute-done.2.refs_8_), channel_id=1, source_target_pairs={{0,1},{1,2},{2,3},{3,0},{16,19},{17,16},{18,17},{19,18},{4,5},{5,6... | collective-permute-start | bytes 1585160 | tf_op jit(solution)/shard_map/ppermute | solution.py:25
  37.6 10.9 %collective-permute-start.7 = (f32[1032,128]{1,0:T(8,128)S(1)}, f32[1032,128]{1,0:T(8,128)S(1)}, u32[]{:S(2)}, u32[]{:S(2)}) collective-permute-start(f32[1032,128]{1,0:T(8,128)S(1)} %collective-permute-done.3.refs_9_), channel_id=1, source_target_pairs={{0,4},{4,8},{8,12},{12,0},{16,28},{20,16},{24,20},{28,24},{1,5},{5... | collective-permute-start | bytes 1585160 | tf_op jit(solution)/shard_map/ppermute | solution.py:25
  42.8 10.4 %collective-permute-start.10 = (f32[1032,128]{1,0:T(8,128)S(1)}, f32[1032,128]{1,0:T(8,128)S(1)}, u32[]{:S(2)}, u32[]{:S(2)}) collective-permute-start(f32[1032,128]{1,0:T(8,128)S(1)} %collective-permute-done.8.refs_3_), channel_id=1, source_target_pairs={{0,1},{1,2},{2,3},{3,0},{16,19},{17,16},{18,17},{19,18},{4,5},{5,6... | collective-permute-start | bytes 1585160 | tf_op jit(solution)/shard_map/ppermute | solution.py:25
  44.0 0.8 copy-start.14
  44.8 10.4 %collective-permute-start.11 = (f32[1032,128]{1,0:T(8,128)S(1)}, f32[1032,128]{1,0:T(8,128)S(1)}, u32[]{:S(2)}, u32[]{:S(2)}) collective-permute-start(f32[1032,128]{1,0:T(8,128)S(1)} %collective-permute-done.9.refs_4_), channel_id=1, source_target_pairs={{0,4},{4,8},{8,12},{12,0},{16,28},{20,16},{24,20},{28,24},{1,5},{5... | collective-permute-start | bytes 1585160 | tf_op jit(solution)/shard_map/ppermute | solution.py:25
  44.8 0.8 copy-start.16
  45.7 0.8 copy-start.6
  46.6 0.8 copy-start.12
  53.3 0.8 copy-start.18
  55.3 0.8 copy-start.20
  56.3 13.4 %collective-permute-start.12 = (f32[1552,128]{1,0:T(8,128)S(1)}, f32[1552,128]{1,0:T(8,128)S(1)}, u32[]{:S(2)}, u32[]{:S(2)}) collective-permute-start(f32[1552,128]{1,0:T(8,128)S(1)} %get-tuple-element.69), channel_id=1, source_target_pairs={{0,1},{1,2},{2,3},{3,0},{16,19},{17,16},{18,17},{19,18},{4,5},{5,6... | collective-permute-start | bytes 2383880 | tf_op jit(solution)/shard_map/ppermute | solution.py:25
  56.8 13.3 %collective-permute-start.13 = (f32[1552,128]{1,0:T(8,128)S(1)}, f32[1552,128]{1,0:T(8,128)S(1)}, u32[]{:S(2)}, u32[]{:S(2)}) collective-permute-start(f32[1552,128]{1,0:T(8,128)S(1)} %get-tuple-element.70), channel_id=1, source_target_pairs={{0,4},{4,8},{8,12},{12,0},{16,28},{20,16},{24,20},{28,24},{1,5},{5... | collective-permute-start | bytes 2383880 | tf_op jit(solution)/shard_map/ppermute | solution.py:25
  56.8 21.4 %collective-permute-start.14 = (f32[1552,128]{1,0:T(8,128)S(1)}, f32[1552,128]{1,0:T(8,128)S(1)}, u32[]{:S(2)}, u32[]{:S(2)}) collective-permute-start(f32[1552,128]{1,0:T(8,128)S(1)} %get-tuple-element.73), channel_id=1, source_target_pairs={{0,1},{1,2},{2,3},{3,0},{16,19},{17,16},{18,17},{19,18},{4,5},{5,6... | collective-permute-start | bytes 2383880 | tf_op jit(solution)/shard_map/ppermute | solution.py:25
  58.3 20.3 %collective-permute-start.15 = (f32[1552,128]{1,0:T(8,128)S(1)}, f32[1552,128]{1,0:T(8,128)}, u32[]{:S(2)}, u32[]{:S(2)}) collective-permute-start(f32[1552,128]{1,0:T(8,128)S(1)} %get-tuple-element.74), channel_id=1, source_target_pairs={{0,4},{4,8},{8,12},{12,0},{16,28},{20,16},{24,20},{28,24},{1,5},{5... | collective-permute-start | bytes 2383880 | tf_op jit(solution)/shard_map/ppermute | solution.py:25
  78.7 3.4 %copy-start = (f32[4096,512]{1,0:T(8,128)S(1)}, f32[4096,512]{1,0:T(8,128)}, u32[]{:S(2)}) copy-start(f32[4096,512]{1,0:T(8,128)} %all-gather.2.cloned.1.call-done.d_ref) | copy-start | bytes 25165828
  82.1 4.4 %copy-start.3 = (f32[1032,128]{1,0:T(8,128)S(1)}, f32[1032,128]{1,0:T(8,128)}, u32[]{:S(2)}) copy-start(f32[1032,128]{1,0:T(8,128)} %copy-done.2) | copy-start | bytes 1585156
  82.1 4.4 %copy-start.5 = (f32[1032,128]{1,0:T(8,128)S(1)}, f32[1032,128]{1,0:T(8,128)}, u32[]{:S(2)}) copy-start(f32[1032,128]{1,0:T(8,128)} %copy-done.4) | copy-start | bytes 1585156
  82.1 4.4 %copy-start.7 = (f32[1032,128]{1,0:T(8,128)S(1)}, f32[1032,128]{1,0:T(8,128)}, u32[]{:S(2)}) copy-start(f32[1032,128]{1,0:T(8,128)} %copy-done.6) | copy-start | bytes 1585156
  82.1 4.4 %copy-start.9 = (f32[1032,128]{1,0:T(8,128)S(1)}, f32[1032,128]{1,0:T(8,128)}, u32[]{:S(2)}) copy-start(f32[1032,128]{1,0:T(8,128)} %copy-done.8) | copy-start | bytes 1585156
  82.1 4.4 %copy-start.11 = (f32[1032,128]{1,0:T(8,128)S(1)}, f32[1032,128]{1,0:T(8,128)}, u32[]{:S(2)}) copy-start(f32[1032,128]{1,0:T(8,128)} %copy-done.10) | copy-start | bytes 1585156
  82.1 4.4 %copy-start.13 = (f32[1032,128]{1,0:T(8,128)S(1)}, f32[1032,128]{1,0:T(8,128)}, u32[]{:S(2)}) copy-start(f32[1032,128]{1,0:T(8,128)} %copy-done.12) | copy-start | bytes 1585156
  82.1 4.4 %copy-start.24 = (f32[1032,128]{1,0:T(8,128)S(1)}, f32[1032,128]{1,0:T(8,128)}, u32[]{:S(2)}) copy-start(f32[1032,128]{1,0:T(8,128)} %copy-done.23) | copy-start | bytes 1585156
  82.1 4.4 %copy-start.26 = (f32[1032,128]{1,0:T(8,128)S(1)}, f32[1032,128]{1,0:T(8,128)}, u32[]{:S(2)}) copy-start(f32[1032,128]{1,0:T(8,128)} %copy-done.25) | copy-start | bytes 1585156
  83.3 13.5 %collective-permute-start.18 = (f32[1552,128]{1,0:T(8,128)S(1)}, f32[1552,128]{1,0:T(8,128)S(1)}, u32[]{:S(2)}, u32[]{:S(2)}) collective-permute-start(f32[1552,128]{1,0:T(8,128)S(1)} %collective-permute-done.12.refs_5_), channel_id=1, source_target_pairs={{0,1},{1,2},{2,3},{3,0},{16,19},{17,16},{18,17},{19,18},{4,5},{5,6... | collective-permute-start | bytes 2383880 | tf_op jit(solution)/shard_map/ppermute | solution.py:25
  85.0 13.3 %collective-permute-start.19 = (f32[1552,128]{1,0:T(8,128)S(1)}, f32[1552,128]{1,0:T(8,128)S(1)}, u32[]{:S(2)}, u32[]{:S(2)}) collective-permute-start(f32[1552,128]{1,0:T(8,128)S(1)} %collective-permute-done.13.refs_6_), channel_id=1, source_target_pairs={{0,4},{4,8},{8,12},{12,0},{16,28},{20,16},{24,20},{28,24},{1,5},{5... | collective-permute-start | bytes 2383880 | tf_op jit(solution)/shard_map/ppermute | solution.py:25
  85.0 20.2 %collective-permute-start.16 = (f32[1552,128]{1,0:T(8,128)S(1)}, f32[1552,128]{1,0:T(8,128)S(1)}, u32[]{:S(2)}, u32[]{:S(2)}) collective-permute-start(f32[1552,128]{1,0:T(8,128)S(1)} %collective-permute-done.14.refs_3_), channel_id=1, source_target_pairs={{0,1},{1,2},{2,3},{3,0},{16,19},{17,16},{18,17},{19,18},{4,5},{5,6... | collective-permute-start | bytes 2383880 | tf_op jit(solution)/shard_map/ppermute | solution.py:25
  86.5 20.3 %collective-permute-start.17 = (f32[1552,128]{1,0:T(8,128)}, f32[1552,128]{1,0:T(8,128)S(1)}, u32[]{:S(2)}, u32[]{:S(2)}) collective-permute-start(f32[1552,128]{1,0:T(8,128)} %collective-permute-done.15.refs_4_), channel_id=1, source_target_pairs={{0,4},{4,8},{8,12},{12,0},{16,28},{20,16},{24,20},{28,24},{1,5},{5... | collective-permute-start | bytes 2383880 | tf_op jit(solution)/shard_map/ppermute | solution.py:25
  86.5 5.8 %copy-start.15 = (f32[1032,128]{1,0:T(8,128)S(1)}, f32[1032,128]{1,0:T(8,128)}, u32[]{:S(2)}) copy-start(f32[1032,128]{1,0:T(8,128)} %copy-done.14) | copy-start | bytes 1585156
  86.5 5.8 %copy-start.17 = (f32[1032,128]{1,0:T(8,128)S(1)}, f32[1032,128]{1,0:T(8,128)}, u32[]{:S(2)}) copy-start(f32[1032,128]{1,0:T(8,128)} %copy-done.16) | copy-start | bytes 1585156
  86.6 5.8 %copy-start.19 = (f32[1032,128]{1,0:T(8,128)S(1)}, f32[1032,128]{1,0:T(8,128)}, u32[]{:S(2)}) copy-start(f32[1032,128]{1,0:T(8,128)} %copy-done.18) | copy-start | bytes 1585156
  86.6 5.8 %copy-start.21 = (f32[1032,128]{1,0:T(8,128)S(1)}, f32[1032,128]{1,0:T(8,128)}, u32[]{:S(2)}) copy-start(f32[1032,128]{1,0:T(8,128)} %copy-done.20) | copy-start | bytes 1585156
  98.3 20.2 %collective-permute-start.22 = (f32[1552,128]{1,0:T(8,128)S(1)}, f32[1552,128]{1,0:T(8,128)S(1)}, u32[]{:S(2)}, u32[]{:S(2)}) collective-permute-start(f32[1552,128]{1,0:T(8,128)S(1)} %collective-permute-done.18.refs_5_), channel_id=1, source_target_pairs={{0,1},{1,2},{2,3},{3,0},{16,19},{17,16},{18,17},{19,18},{4,5},{5,6... | collective-permute-start | bytes 2383880 | tf_op jit(solution)/shard_map/ppermute | solution.py:25
  99.8 18.7 %collective-permute-start.23 = (f32[1552,128]{1,0:T(8,128)S(1)}, f32[1552,128]{1,0:T(8,128)S(1)}, u32[]{:S(2)}, u32[]{:S(2)}) collective-permute-start(f32[1552,128]{1,0:T(8,128)S(1)} %collective-permute-done.19.refs_6_), channel_id=1, source_target_pairs={{0,4},{4,8},{8,12},{12,0},{16,28},{20,16},{24,20},{28,24},{1,5},{5... | collective-permute-start | bytes 2383880 | tf_op jit(solution)/shard_map/ppermute | solution.py:25
  106.8 15.5 %collective-permute-start.20 = (f32[1552,128]{1,0:T(8,128)S(1)}, f32[1552,128]{1,0:T(8,128)S(1)}, u32[]{:S(2)}, u32[]{:S(2)}) collective-permute-start(f32[1552,128]{1,0:T(8,128)S(1)} %collective-permute-done.16.refs_3_), channel_id=1, source_target_pairs={{0,1},{1,2},{2,3},{3,0},{16,19},{17,16},{18,17},{19,18},{4,5},{5,6... | collective-permute-start | bytes 2383880 | tf_op jit(solution)/shard_map/ppermute | solution.py:25
  108.3 15.5 %collective-permute-start.21 = (f32[1552,128]{1,0:T(8,128)S(1)}, f32[1552,128]{1,0:T(8,128)S(1)}, u32[]{:S(2)}, u32[]{:S(2)}) collective-permute-start(f32[1552,128]{1,0:T(8,128)S(1)} %collective-permute-done.17.refs_4_), channel_id=1, source_target_pairs={{0,4},{4,8},{8,12},{12,0},{16,28},{20,16},{24,20},{28,24},{1,5},{5... | collective-permute-start | bytes 2383880 | tf_op jit(solution)/shard_map/ppermute | solution.py:25
Sparse Core Ops, SparseCore 0:
  10.2 52.3 all-gather.1

commit v2 on v1

v2 whole, which is shorter than its diff:
```python
import functools

import jax
import jax.numpy as jnp
from jax import lax
from jax.experimental import pallas as pl
from jax.experimental.pallas import tpu as pltpu
from jax.sharding import Mesh, PartitionSpec as P

MBL = 16
KB = 32
NY = 4
NX = 4
HALF = 8
MARK = 8
MIB = 2**20


def ring(v, axis, n):
    perm = []
    for q, step in ((0, 1), (1, -1)):
        for i in range(n):
            at = [(j * 2 + q if axis == "z" else q * n + j) for j in (i, (i + step) % n)]
            perm.append(tuple(at))
    return lax.ppermute(v, ("z", "core") if axis == "z" else ("core", axis), perm)


def step_both(pair):
    return lax.optimization_barrier((ring(pair[0], "x", NX), ring(pair[1], "y", NY)))


def prepare_kernel(index, mask, tiles_ref, d_ref, a_ref, b_ref, masked_ref, d_buf, sem):
    data = HALF * a_ref.shape[1]
    size = d_ref.shape[0] // mask.shape[0]
    copies = [
        pltpu.make_async_copy(d_ref, d_buf, sem.at[0]),
        pltpu.make_async_copy(tiles_ref.at[pl.ds(0, data), :], a_ref.at[pl.ds(0, data), :], sem.at[1]),
        pltpu.make_async_copy(tiles_ref.at[pl.ds(data, data), :], b_ref.at[pl.ds(0, data), :], sem.at[2]),
    ]
    for c in copies:
        c.start()
    lane = lax.broadcasted_iota(jnp.int32, (MARK, a_ref.shape[1]), 1)
    for n, ref in enumerate((a_ref, b_ref)):
        places = jnp.zeros(lane.shape, jnp.int32)
        for j in range(HALF):
            places = jnp.where(lane == j, index[n * HALF + j], places)
        ref[data:, :] = places.astype(jnp.float32)
    copies[0].wait()
    for i in range(mask.shape[0]):
        for j in range(mask.shape[1]):
            block = slice(i * size, (i + 1) * size), slice(j * size, (j + 1) * size)
            masked_ref[block] = d_buf[block] * mask[i, j].astype(jnp.float32)
    copies[1].wait()
    copies[2].wait()


def prepare(a_tiles, index, d, mask):
    stored, size = a_tiles.shape[0], a_tiles.shape[1]
    smem = pl.BlockSpec(memory_space=pltpu.SMEM)
    vmem = pl.BlockSpec(memory_space=pltpu.VMEM)
    payload = pltpu.VMEM((HALF * size + MARK, size), jnp.float32)
    hbm = [pltpu.with_memory_space_constraint(v, pltpu.HBM) for v in (a_tiles.reshape(stored * size, size), d)]
    return pl.pallas_call(
        prepare_kernel,
        in_specs=[smem, smem] + [pl.BlockSpec(memory_space=pltpu.HBM)] * 2,
        out_specs=[vmem] * 3,
        out_shape=[payload, payload, pltpu.VMEM(d.shape, jnp.float32)],
        scratch_shapes=[pltpu.VMEM(d.shape, jnp.float32), pltpu.SemaphoreType.DMA((3,))],
        compiler_params=pltpu.CompilerParams(vmem_limit_bytes=8 * MIB),
        cost_estimate=pl.CostEstimate(flops=d.size, bytes_accessed=16 * d.size, transcendentals=0),
    )(index, mask, *hbm)


def after(pair, others):
    return lax.optimization_barrier((*pair, *others))[: len(pair)]


def split_kernel(d_ref, hi_ref, lo_ref, d_buf, sem):
    parts = sem.shape[0]
    rows = d_ref.shape[0] // parts
    at = [pl.ds(i * rows, rows) for i in range(parts)]
    copies = [pltpu.make_async_copy(d_ref.at[r, :], d_buf.at[r, :], sem.at[i]) for i, r in enumerate(at)]
    for c in copies:
        c.start()
    for c, r in zip(copies, at):
        c.wait()
        d = d_buf[r, :]
        hi = d.astype(jnp.bfloat16)
        hi_ref[r, :] = hi
        lo_ref[r, :] = (d - hi.astype(jnp.float32)).astype(jnp.bfloat16)


def split(d):
    rows, width = d.shape
    vmem = pl.BlockSpec(memory_space=pltpu.VMEM)
    return pl.pallas_call(
        split_kernel,
        in_specs=[pl.BlockSpec(memory_space=pltpu.HBM)],
        out_specs=[vmem, vmem],
        out_shape=[pltpu.VMEM(d.shape, jnp.bfloat16)] * 2,
        scratch_shapes=[pltpu.VMEM(d.shape, jnp.float32), pltpu.SemaphoreType.DMA((8,))],
        compiler_params=pltpu.CompilerParams(vmem_limit_bytes=20 * MIB),
        cost_estimate=pl.CostEstimate(
            flops=4 * rows * width, bytes_accessed=8 * rows * width, transcendentals=0
        ),
    )(pltpu.with_memory_space_constraint(d, pltpu.HBM))


def add_kernel(marks, first, last, size, *refs):
    n = len(marks)
    operands, refs = refs[: 2 + n + (not first)], refs[2 + n + (not first) :]
    acc = None if first else operands[0]
    hi_ref, lo_ref, *tiles = operands[not first :]
    out, places, sem = refs[0], refs[1 : 1 + n], refs[1 + n]
    copies = [
        pltpu.make_async_copy(t.at[pl.ds(len(m) * size, p.shape[0]), :], p, sem.at[i])
        for i, (t, m, p) in enumerate(zip(tiles, marks, places))
    ]
    for c in copies:
        c.start()
    for c in copies:
        c.wait()
    todo = [(i, m) for i, mark in enumerate(marks) for m in range(len(mark))]
    group = 16 if len(todo) % 16 == 0 else 12

    def add_columns(out, columns):
        out[...] = jnp.zeros_like(out) if first else acc[:, columns]
        for at in range(0, len(todo), group):
            products = []
            for i, m in todo[at : at + group]:
                place = places[i][marks[i][m]].astype(jnp.int32)
                k = pl.multiple_of((place & (KB - 1)) * size, size)
                t = tiles[i][m * size : (m + 1) * size, :]
                hi = t.astype(jnp.bfloat16)
                lo = (t - hi.astype(jnp.float32)).astype(jnp.bfloat16)
                dhi = hi_ref[pl.ds(k, size), columns]
                dlo = lo_ref[pl.ds(k, size), columns]
                product = jnp.dot(
                    jnp.concatenate([hi, lo], axis=1),
                    jnp.concatenate([dhi, dhi], axis=0),
                    preferred_element_type=jnp.float32,
                ) + jnp.dot(hi, dlo, preferred_element_type=jnp.float32)
                products.append(((place // KB) & (MBL - 1), product))
            for r, product in products:
                out[pl.ds(pl.multiple_of(r * size, size), size), :] += product

    width = hi_ref.shape[1]
    if not last:
        add_columns(out, slice(0, width))
        return
    buffers, out_sem = refs[2 + n : -1], refs[-1]
    part = width // len(buffers)
    writes = []
    for h, buffer in enumerate(buffers):
        add_columns(buffer, slice(h * part, (h + 1) * part))
        write = pltpu.make_async_copy(buffer, out.at[:, pl.ds(h * part, part)], out_sem.at[h])
        write.start()
        writes.append(write)
    for write in writes:
        write.wait()


def add_products(acc, hi, lo, tiles, marks, last=False):
    size = tiles[0].shape[1]
    depth, width = hi.shape
    first = acc is None
    vmem = pl.BlockSpec(memory_space=pltpu.VMEM)
    operands = ([] if first else [acc]) + [hi, lo, *tiles]
    total = sum(len(m) for m in marks)
    shape = (MBL * size, width)
    scratch = [pltpu.SMEM((t.shape[0] - len(m) * size, size), jnp.float32) for t, m in zip(tiles, marks)]
    scratch.append(pltpu.SemaphoreType.DMA((len(tiles),)))
    if last:
        scratch += [pltpu.VMEM((shape[0], width // 2), jnp.float32)] * 2 + [pltpu.SemaphoreType.DMA((2,))]
    return pl.pallas_call(
        functools.partial(add_kernel, marks, first, last, size),
        in_specs=[vmem] * len(operands),
        out_specs=pl.BlockSpec(memory_space=pltpu.HBM) if last else vmem,
        out_shape=jax.ShapeDtypeStruct(shape, jnp.float32) if last else pltpu.VMEM(shape, jnp.float32),
        input_output_aliases={} if first or last else {0: 0},
        scratch_shapes=scratch,
        compiler_params=pltpu.CompilerParams(vmem_limit_bytes=24 * MIB),
        cost_estimate=pl.CostEstimate(
            flops=total * size * size * width * 12,
            bytes_accessed=total * size * size * 4,
            transcendentals=0,
        ),
    )(*operands)


def body(a_tiles, a_index, d_values, d_mask):
    stored, size = a_tiles.shape[0], a_tiles.shape[1]
    few = HALF // 2
    data = HALF * size
    a, b, masked = prepare(a_tiles, a_index, d_values, d_mask)
    density = lax.all_gather(masked, ("z", "core"), axis=0, tiled=True)

    whole = [(0, j) for j in range(HALF)]

    def early(u, v):
        return jnp.concatenate([u[:data], v[: data // 2], u[data:], v[data:]])

    early_marks = whole + [(MARK, j) for j in range(few)]

    def late(u, v):
        return jnp.concatenate([u[data // 2 : data], v[:data], u[data:], v[data:]])

    late_marks = [(0, j) for j in range(few, HALF)] + [(MARK, j) for j in range(HALF)]

    p1 = step_both((a, b))
    q1 = step_both((b, a))
    p2 = step_both(p1)
    q2 = step_both(after(q1, p1))
    (a1, b1), (a2, b2) = p1, p2
    p3 = after(p2, q1)
    a3, b3, u, v = lax.optimization_barrier(
        (ring(p3[0], "x", NX), ring(p3[1], "y", NY), early(b1, b2), early(a1, a2))
    )
    p3 = a3, b3
    q3 = step_both(after(q2, p2))
    p4 = step_both(after((u, v), q2))
    *p4, density, q3x, q3y = lax.optimization_barrier((*p4, density, *q3))
    q3 = q3x, q3y
    hi, lo = split(density)
    *q4, hi, lo = lax.optimization_barrier((late(b2, b3), late(a2, a3), hi, lo))
    q4 = step_both(q4)

    def add(acc, pairs, marks, **kw):
        tiles = [t for pair in pairs for t in pair]
        return add_products(acc, hi, lo, tiles, [m for m in marks for _ in range(2)], **kw)

    p5 = step_both(p4)
    q5 = step_both(q4)
    p6 = step_both(p5)
    q6 = step_both(q5)
    acc = add(None, [(a, b), p1, q1, p2], [whole] * 4)
    acc = add(acc, [q2, p3, q3], [whole] * 3)
    acc = add(acc, [p4, q4], [early_marks, late_marks])
    acc = add(acc, [p5, q5, p6], [early_marks, late_marks, early_marks])
    return add(acc, [q6], [late_marks], last=True)


def solution(mesh):
    grid = Mesh(mesh.devices.reshape(-1, 2, NY, NX), ("z", "core", "y", "x"))
    row, col = ("z", "core"), ("y", "x")
    in_specs = (P(row + col, None, None), P(row + col), P(row, col), P(row, col))
    return jax.shard_map(
        body, mesh=grid, in_specs=in_specs, out_specs=P(row, col), check_vma=False
    )
```

time: 137 us -> 128 us (0.934)
  local copies, waits for them, and re-layouts: 14.2 us -> 1.68 us
  waiting for transfers between devices: 57.7 us -> 50.9 us
  Pallas kernels: 29.8 us -> 34.7 us
  starting transfers between devices: 20.8 us -> 24.9 us
    unnamed x54 -> x52, local copies, waits for them, and re-layouts: 12.6 us -> 1.43 us
    ppermute x24, waiting for transfers between devices: 57.7 us -> 48.2 us  [ring(): lax.ppermute(v, ('z', 'core') if axis == 'z' else ('core', axis), perm)]
    pallas_call x7, Pallas kernels: 29.8 us -> 34.7 us  [the longest x5 27.9 us: add_products(): pl.pallas_call(functools.partial(add_kernel, marks, first, last, size), i...]
    ppermute x24, starting transfers between devices: 20.8 us -> 24.9 us  [ring(): lax.ppermute(v, ('z', 'core') if axis == 'z' else ('core', axis), perm)]
    all_gather x1, waiting for transfers between devices: 0.01 us -> 2.66 us  [body(): density = lax.all_gather(masked, ('z', 'core'), axis=0, tiled=True)]
    concatenate x2, other arithmetic: 0.08 us -> 2 us  [late(): return jnp.concatenate([u[data // 2:data], v[:data], u[data:], v[data:]])]
  transfers between devices with their start and end apart: 25 -> 25, of which waited for: 19 -> 21; matrix products, arithmetic and copies ran while one was open for 2% -> 2% of each run, Pallas kernels for 15% -> 18%
where the time goes in v2:
time: 128 us
  waiting for transfers between devices  50.9 us (40%)
  Pallas kernels  34.7 us (27%)
  starting transfers between devices  24.9 us (19%)
  between operations  13.7 us (11%)
  other arithmetic  2.1 us (2%)
  local copies, waits for them, and re-layouts  1.68 us (1%)
    ppermute x24, waiting for transfers between devices, ring(): lax.ppermute(v, ('z', 'core') if axis == 'z' else ('core', axis), perm)  48.2 us
    pallas_call x5, Pallas kernels, add_products(): pl.pallas_call(functools.partial(add_kernel, marks, first, last, size), i...  27.9 us
    ppermute x24, starting transfers between devices, ring(): lax.ppermute(v, ('z', 'core') if axis == 'z' else ('core', axis), perm)  24.9 us
    pallas_call x1, Pallas kernels, split(): pl.pallas_call(split_kernel, in_specs=[pl.BlockSpec(memory_space=pltpu.HB...  3.76 us
    pallas_call x1, Pallas kernels, prepare(): pl.pallas_call(prepare_kernel, in_specs=[smem, smem] + [pl.BlockSpec(memo...  3.08 us
    all_gather x1, waiting for transfers between devices, body(): density = lax.all_gather(masked, ('z', 'core'), axis=0, tiled=True)  2.66 us
  transfers between devices with their start and end apart: 25, of which 21 were waited for; matrix products, arithmetic and copies ran while one was open for 2% of the time, Pallas kernels for 18%

profile of v2, /device:TPU:0, one launch (start us, length us, event | category | flops | bytes accessed | tf_op | source)
XLA Modules:
  0.0 128.0 jit_solution(15455456446592880398)
XLA Ops:
  6.5 0.7 copy-done.14
  7.2 0.7 copy-done.15
  7.9 3.1 %shard_map.46 = (f32[1032,128]{1,0:T(8,128)S(1)}, f32[1032,128]{1,0:T(8,128)S(1)}, f32[512,512]{1,0:T(8,128)}) custom-call(s32[16]{0:T(128)S(1)} %copy-done.15, s32[4,4]{1,0:T(4,128)S(1)} %copy-done.14, f32[2048,128]{1,0:T(8,128)} %bitcast.1, f32[512,512]{1,0:T(8,128)} %d_ref.1), custom_call_target="tpu_custom_call" | custom-call | flops 262144 | bytes 4194304 | tf_op jit(solution)/shard_map/pallas_call | solution.py:63
  11.0 0.0 all-gather.2.cloned.1.call-update
  11.0 1.6 %collective-permute-start = (f32[1032,128]{1,0:T(8,128)S(1)}, f32[1032,128]{1,0:T(8,128)S(1)}, u32[]{:S(2)}, u32[]{:S(2)}) collective-permute-start(f32[1032,128]{1,0:T(8,128)S(1)} %get-tuple-element.53.refs_2_), channel_id=1, source_target_pairs={{0,1},{1,2},{2,3},{3,0},{16,19},{17,16},{18,17},{19,18},{4,5},{5,6... | collective-permute-start | bytes 1585160 | tf_op jit(solution)/shard_map/ppermute | solution.py:25
  12.6 1.6 %collective-permute-start.1 = (f32[1032,128]{1,0:T(8,128)S(1)}, f32[1032,128]{1,0:T(8,128)S(1)}, u32[]{:S(2)}, u32[]{:S(2)}) collective-permute-start(f32[1032,128]{1,0:T(8,128)S(1)} %get-tuple-element.54.refs_3_), channel_id=1, source_target_pairs={{0,4},{4,8},{8,12},{12,0},{16,28},{20,16},{24,20},{28,24},{1,5},{5... | collective-permute-start | bytes 1585160 | tf_op jit(solution)/shard_map/ppermute | solution.py:25
  14.2 1.6 %collective-permute-start.5 = (f32[1032,128]{1,0:T(8,128)S(1)}, f32[1032,128]{1,0:T(8,128)S(1)}, u32[]{:S(2)}, u32[]{:S(2)}) collective-permute-start(f32[1032,128]{1,0:T(8,128)S(1)} %get-tuple-element.53.refs_2_), channel_id=1, source_target_pairs={{0,4},{4,8},{8,12},{12,0},{16,28},{20,16},{24,20},{28,24},{1,5},{5... | collective-permute-start | bytes 1585160 | tf_op jit(solution)/shard_map/ppermute | solution.py:25
  15.8 1.5 %collective-permute-start.4 = (f32[1032,128]{1,0:T(8,128)S(1)}, f32[1032,128]{1,0:T(8,128)S(1)}, u32[]{:S(2)}, u32[]{:S(2)}) collective-permute-start(f32[1032,128]{1,0:T(8,128)S(1)} %get-tuple-element.54.refs_3_), channel_id=1, source_target_pairs={{0,1},{1,2},{2,3},{3,0},{16,19},{17,16},{18,17},{19,18},{4,5},{5,6... | collective-permute-start | bytes 1585160 | tf_op jit(solution)/shard_map/ppermute | solution.py:25
  17.3 4.2 %collective-permute-done.refs_4_ = f32[1032,128]{1,0:T(8,128)S(1)} collective-permute-done((f32[1032,128]{1,0:T(8,128)S(1)}, f32[1032,128]{1,0:T(8,128)S(1)}, u32[]{:S(2)}, u32[]{:S(2)}) %collective-permute-start) | collective-permute-done | bytes 528416 | tf_op jit(solution)/shard_map/ppermute | solution.py:25
  21.5 1.6 %collective-permute-done.1.refs_5_ = f32[1032,128]{1,0:T(8,128)S(1)} collective-permute-done((f32[1032,128]{1,0:T(8,128)S(1)}, f32[1032,128]{1,0:T(8,128)S(1)}, u32[]{:S(2)}, u32[]{:S(2)}) %collective-permute-start.1) | collective-permute-done | bytes 528416 | tf_op jit(solution)/shard_map/ppermute | solution.py:25
  23.1 1.5 %collective-permute-start.2 = (f32[1032,128]{1,0:T(8,128)S(1)}, f32[1032,128]{1,0:T(8,128)S(1)}, u32[]{:S(2)}, u32[]{:S(2)}) collective-permute-start(f32[1032,128]{1,0:T(8,128)S(1)} %collective-permute-done.refs_4_), channel_id=1, source_target_pairs={{0,1},{1,2},{2,3},{3,0},{16,19},{17,16},{18,17},{19,18},{4,5},{5,6... | collective-permute-start | bytes 1585160 | tf_op jit(solution)/shard_map/ppermute | solution.py:25
  24.6 0.4 collective-permute-start.3
  24.9 3.8 %collective-permute-done.5.refs_7_ = f32[1032,128]{1,0:T(8,128)S(1)} collective-permute-done((f32[1032,128]{1,0:T(8,128)S(1)}, f32[1032,128]{1,0:T(8,128)S(1)}, u32[]{:S(2)}, u32[]{:S(2)}) %collective-permute-start.5) | collective-permute-done | bytes 528416 | tf_op jit(solution)/shard_map/ppermute | solution.py:25
  28.7 0.0 collective-permute-done.4.refs_6_
  28.8 1.6 %collective-permute-start.8 = (f32[1032,128]{1,0:T(8,128)S(1)}, f32[1032,128]{1,0:T(8,128)S(1)}, u32[]{:S(2)}, u32[]{:S(2)}) collective-permute-start(f32[1032,128]{1,0:T(8,128)S(1)} %collective-permute-done.4.refs_6_), channel_id=1, source_target_pairs={{0,1},{1,2},{2,3},{3,0},{16,19},{17,16},{18,17},{19,18},{4,5},{5,6... | collective-permute-start | bytes 1585160 | tf_op jit(solution)/shard_map/ppermute | solution.py:25
  30.3 0.4 collective-permute-start.9
  30.8 2.8 %collective-permute-done.2.refs_8_ = f32[1032,128]{1,0:T(8,128)S(1)} collective-permute-done((f32[1032,128]{1,0:T(8,128)S(1)}, f32[1032,128]{1,0:T(8,128)S(1)}, u32[]{:S(2)}, u32[]{:S(2)}) %collective-permute-start.2) | collective-permute-done | bytes 528416 | tf_op jit(solution)/shard_map/ppermute | solution.py:25
  33.5 1.5 %collective-permute-done.3.refs_9_ = f32[1032,128]{1,0:T(8,128)S(1)} collective-permute-done((f32[1032,128]{1,0:T(8,128)S(1)}, f32[1032,128]{1,0:T(8,128)S(1)}, u32[]{:S(2)}, u32[]{:S(2)}) %collective-permute-start.3) | collective-permute-done | bytes 528416 | tf_op jit(solution)/shard_map/ppermute | solution.py:25
  35.0 1.2 collective-permute-start.6
  36.2 0.1 collective-permute-start.7
  36.3 0.1 fusion
  36.4 2.9 %collective-permute-done.8.refs_3_ = f32[1032,128]{1,0:T(8,128)S(1)} collective-permute-done((f32[1032,128]{1,0:T(8,128)S(1)}, f32[1032,128]{1,0:T(8,128)S(1)}, u32[]{:S(2)}, u32[]{:S(2)}) %collective-permute-start.8) | collective-permute-done | bytes 528416 | tf_op jit(solution)/shard_map/ppermute | solution.py:25
  39.3 1.5 %collective-permute-done.9.refs_4_ = f32[1032,128]{1,0:T(8,128)S(1)} collective-permute-done((f32[1032,128]{1,0:T(8,128)S(1)}, f32[1032,128]{1,0:T(8,128)S(1)}, u32[]{:S(2)}, u32[]{:S(2)}) %collective-permute-start.9) | collective-permute-done | bytes 528416 | tf_op jit(solution)/shard_map/ppermute | solution.py:25
  40.8 1.2 collective-permute-start.12
  41.9 0.0 collective-permute-start.13
  42.0 0.1 pad_maximum_fusion.1
  42.0 0.1 pad_maximum_fusion
  42.1 3.4 %collective-permute-done.6.refs_5_ = f32[1032,128]{1,0:T(8,128)S(1)} collective-permute-done((f32[1032,128]{1,0:T(8,128)S(1)}, f32[1032,128]{1,0:T(8,128)S(1)}, u32[]{:S(2)}, u32[]{:S(2)}) %collective-permute-start.6) | collective-permute-done | bytes 528416 | tf_op jit(solution)/shard_map/ppermute | solution.py:25
  45.5 1.2 collective-permute-done.7.refs_6_
  46.7 1.0 collective-permute-start.10
  47.6 0.0 collective-permute-start.11
  47.7 3.5 %collective-permute-done.12.refs_7_ = f32[1032,128]{1,0:T(8,128)S(1)} collective-permute-done((f32[1032,128]{1,0:T(8,128)S(1)}, f32[1032,128]{1,0:T(8,128)S(1)}, u32[]{:S(2)}, u32[]{:S(2)}) %collective-permute-start.12) | collective-permute-done | bytes 528416 | tf_op jit(solution)/shard_map/ppermute | solution.py:25
  51.2 1.2 collective-permute-done.13.refs_8_
  52.4 1.0 pad_maximum_fusion.2
  53.4 1.0 pad_maximum_fusion.3
  54.4 5.6 %collective-permute-done.10.refs_3_ = f32[1552,128]{1,0:T(8,128)S(1)} collective-permute-done((f32[1552,128]{1,0:T(8,128)S(1)}, f32[1552,128]{1,0:T(8,128)S(1)}, u32[]{:S(2)}, u32[]{:S(2)}) %collective-permute-start.10) | collective-permute-done | bytes 794656 | tf_op jit(solution)/shard_map/ppermute | solution.py:25
  59.9 1.0 collective-permute-done.11.refs_4_
  60.9 2.7 %all-gather.2.cloned.1.call-done.d_ref = f32[4096,512]{1,0:T(8,128)} async-done(((f32[512,512]{1,0:T(8,128)}), f32[4096,512]{1,0:T(8,128)}) %all-gather.2.cloned.1.call-update) | async-done | bytes 8388624 | tf_op jit(solution)/shard_map/all_gather | solution.py:196
  63.6 3.8 %shard_map.47 = (bf16[4096,512]{1,0:T(8,128)(2,1)S(1)}, bf16[4096,512]{1,0:T(8,128)(2,1)S(1)}) custom-call(f32[4096,512]{1,0:T(8,128)} %all-gather.2.cloned.1.call-done.d_ref), custom_call_target="tpu_custom_call" | custom-call | flops 8388608 | bytes 16777216 | tf_op jit(solution)/shard_map/pallas_call | solution.py:96
  67.4 1.5 %collective-permute-start.14 = (f32[1552,128]{1,0:T(8,128)S(1)}, f32[1552,128]{1,0:T(8,128)S(1)}, u32[]{:S(2)}, u32[]{:S(2)}) collective-permute-start(f32[1552,128]{1,0:T(8,128)S(1)} %copy-done.24), channel_id=1, source_target_pairs={{0,1},{1,2},{2,3},{3,0},{16,19},{17,16},{18,17},{19,18},{4,5},{5,6... | collective-permute-start | bytes 2383880 | tf_op jit(solution)/shard_map/ppermute | solution.py:25
  69.0 1.5 %collective-permute-start.15 = (f32[1552,128]{1,0:T(8,128)S(1)}, f32[1552,128]{1,0:T(8,128)S(1)}, u32[]{:S(2)}, u32[]{:S(2)}) collective-permute-start(f32[1552,128]{1,0:T(8,128)S(1)} %copy-done.25), channel_id=1, source_target_pairs={{0,4},{4,8},{8,12},{12,0},{16,28},{20,16},{24,20},{28,24},{1,5},{5... | collective-permute-start | bytes 2383880 | tf_op jit(solution)/shard_map/ppermute | solution.py:25
  70.5 1.5 %collective-permute-start.16 = (f32[1552,128]{1,0:T(8,128)S(1)}, f32[1552,128]{1,0:T(8,128)S(1)}, u32[]{:S(2)}, u32[]{:S(2)}) collective-permute-start(f32[1552,128]{1,0:T(8,128)S(1)} %collective-permute-done.10.refs_3_), channel_id=1, source_target_pairs={{0,1},{1,2},{2,3},{3,0},{16,19},{17,16},{18,17},{19,18},{4,5},{5,6... | collective-permute-start | bytes 2383880 | tf_op jit(solution)/shard_map/ppermute | solution.py:25
  71.9 1.5 %collective-permute-start.17 = (f32[1552,128]{1,0:T(8,128)S(1)}, f32[1552,128]{1,0:T(8,128)S(1)}, u32[]{:S(2)}, u32[]{:S(2)}) collective-permute-start(f32[1552,128]{1,0:T(8,128)S(1)} %collective-permute-done.11.refs_4_), channel_id=1, source_target_pairs={{0,4},{4,8},{8,12},{12,0},{16,28},{20,16},{24,20},{28,24},{1,5},{5... | collective-permute-start | bytes 2383880 | tf_op jit(solution)/shard_map/ppermute | solution.py:25
  73.4 7.4 %collective-permute-done.14.refs_5_ = f32[1552,128]{1,0:T(8,128)S(1)} collective-permute-done((f32[1552,128]{1,0:T(8,128)S(1)}, f32[1552,128]{1,0:T(8,128)S(1)}, u32[]{:S(2)}, u32[]{:S(2)}) %collective-permute-start.14) | collective-permute-done | bytes 794656 | tf_op jit(solution)/shard_map/ppermute | solution.py:25
  80.8 1.5 %collective-permute-done.15.refs_6_ = f32[1552,128]{1,0:T(8,128)S(1)} collective-permute-done((f32[1552,128]{1,0:T(8,128)S(1)}, f32[1552,128]{1,0:T(8,128)S(1)}, u32[]{:S(2)}, u32[]{:S(2)}) %collective-permute-start.15) | collective-permute-done | bytes 794656 | tf_op jit(solution)/shard_map/ppermute | solution.py:25
  82.3 1.5 %collective-permute-start.18 = (f32[1552,128]{1,0:T(8,128)S(1)}, f32[1552,128]{1,0:T(8,128)S(1)}, u32[]{:S(2)}, u32[]{:S(2)}) collective-permute-start(f32[1552,128]{1,0:T(8,128)S(1)} %collective-permute-done.14.refs_5_), channel_id=1, source_target_pairs={{0,1},{1,2},{2,3},{3,0},{16,19},{17,16},{18,17},{19,18},{4,5},{5,6... | collective-permute-start | bytes 2383880 | tf_op jit(solution)/shard_map/ppermute | solution.py:25
  83.7 0.3 collective-permute-start.19
  84.0 5.9 %shard_map.48.refs_0_ = f32[2048,512]{1,0:T(8,128)S(1)} custom-call(bf16[4096,512]{1,0:T(8,128)(2,1)S(1)} %get-tuple-element.83.refs_0_.refs_1_, bf16[4096,512]{1,0:T(8,128)(2,1)S(1)} %get-tuple-element.84.refs_1_.refs_2_, f32[1032,128]{1,0:T(8,128)S(1)} %copy-done.17, f32[1032,128]{1,0:T(8,128)S(1)} %copy-done.19, ...), custom_call_target="tpu_custom_call" | custom-call | flops 6442450944 | bytes 4194304 | tf_op jit(solution)/shard_map/pallas_call | solution.py:175
  90.0 0.0 collective-permute-done.16.refs_3_
  90.0 0.8 collective-permute-done.17.refs_4_
  90.8 1.5 %collective-permute-start.20 = (f32[1552,128]{1,0:T(8,128)S(1)}, f32[1552,128]{1,0:T(8,128)S(1)}, u32[]{:S(2)}, u32[]{:S(2)}) collective-permute-start(f32[1552,128]{1,0:T(8,128)S(1)} %collective-permute-done.16.refs_3_), channel_id=1, source_target_pairs={{0,1},{1,2},{2,3},{3,0},{16,19},{17,16},{18,17},{19,18},{4,5},{5,6... | collective-permute-start | bytes 2383880 | tf_op jit(solution)/shard_map/ppermute | solution.py:25
  92.2 0.5 collective-permute-start.21
  92.8 5.0 %shard_map.49.refs_0_ = f32[2048,512]{1,0:T(8,128)S(1)} custom-call(f32[2048,512]{1,0:T(8,128)S(1)} %shard_map.48.refs_0_, bf16[4096,512]{1,0:T(8,128)(2,1)S(1)} %get-tuple-element.83.refs_0_.refs_1_, bf16[4096,512]{1,0:T(8,128)(2,1)S(1)} %get-tuple-element.84.refs_1_.refs_2_, f32[1032,128]{1,0:T(8,128)S(1)} %copy-done.7, ...), custom_call_target="tpu_custom_call", output_to_operand_aliasing={{}: (0, {})} | custom-call | flops 4831838208 | bytes 3145728 | tf_op jit(solution)/shard_map/pallas_call | solution.py:175
  97.8 0.0 collective-permute-done.18.refs_5_
  97.8 1.5 %collective-permute-done.19.refs_6_ = f32[1552,128]{1,0:T(8,128)S(1)} collective-permute-done((f32[1552,128]{1,0:T(8,128)S(1)}, f32[1552,128]{1,0:T(8,128)S(1)}, u32[]{:S(2)}, u32[]{:S(2)}) %collective-permute-start.19) | collective-permute-done | bytes 794656 | tf_op jit(solution)/shard_map/ppermute | solution.py:25
  99.3 1.5 %collective-permute-start.22 = (f32[1552,128]{1,0:T(8,128)S(1)}, f32[1552,128]{1,0:T(8,128)S(1)}, u32[]{:S(2)}, u32[]{:S(2)}) collective-permute-start(f32[1552,128]{1,0:T(8,128)S(1)} %collective-permute-done.18.refs_5_), channel_id=1, source_target_pairs={{0,1},{1,2},{2,3},{3,0},{16,19},{17,16},{18,17},{19,18},{4,5},{5,6... | collective-permute-start | bytes 2383880 | tf_op jit(solution)/shard_map/ppermute | solution.py:25
  100.8 0.3 collective-permute-start.23
  101.0 5.1 %shard_map.50.refs_0_ = f32[2048,512]{1,0:T(8,128)S(1)} custom-call(f32[2048,512]{1,0:T(8,128)S(1)} %shard_map.49.refs_0_, bf16[4096,512]{1,0:T(8,128)(2,1)S(1)} %get-tuple-element.83.refs_0_.refs_1_, bf16[4096,512]{1,0:T(8,128)(2,1)S(1)} %get-tuple-element.84.refs_1_.refs_2_, ...), custom_call_target="tpu_custom_call", output_to_operand_aliasing={{}: (0, {})} | custom-call | flops 4831838208 | bytes 3145728 | tf_op jit(solution)/shard_map/pallas_call | solution.py:175
  106.1 0.2 collective-permute-done.20.refs_7_
  106.3 1.5 %collective-permute-done.21.refs_8_ = f32[1552,128]{1,0:T(8,128)S(1)} collective-permute-done((f32[1552,128]{1,0:T(8,128)S(1)}, f32[1552,128]{1,0:T(8,128)S(1)}, u32[]{:S(2)}, u32[]{:S(2)}) %collective-permute-start.21) | collective-permute-done | bytes 794656 | tf_op jit(solution)/shard_map/ppermute | solution.py:25
  107.8 7.0 %shard_map.51.refs_0_ = f32[2048,512]{1,0:T(8,128)S(1)} custom-call(f32[2048,512]{1,0:T(8,128)S(1)} %shard_map.50.refs_0_, bf16[4096,512]{1,0:T(8,128)(2,1)S(1)} %get-tuple-element.83.refs_0_.refs_1_, bf16[4096,512]{1,0:T(8,128)(2,1)S(1)} %get-tuple-element.84.refs_1_.refs_2_, ...), custom_call_target="tpu_custom_call", output_to_operand_aliasing={{}: (0, {})} | custom-call | flops 7247757312 | bytes 4718592 | tf_op jit(solution)/shard_map/pallas_call | solution.py:175
  114.8 0.0 collective-permute-done.22.refs_3_
  114.8 1.5 %collective-permute-done.23.refs_4_ = f32[1552,128]{1,0:T(8,128)S(1)} collective-permute-done((f32[1552,128]{1,0:T(8,128)S(1)}, f32[1552,128]{1,0:T(8,128)S(1)}, u32[]{:S(2)}, u32[]{:S(2)}) %collective-permute-start.23) | collective-permute-done | bytes 794656 | tf_op jit(solution)/shard_map/ppermute | solution.py:25
  116.3 4.8 %shard_map.52 = f32[2048,512]{1,0:T(8,128)} custom-call(f32[2048,512]{1,0:T(8,128)S(1)} %shard_map.51.refs_0_, bf16[4096,512]{1,0:T(8,128)(2,1)S(1)} %get-tuple-element.83.refs_0_.refs_1_, bf16[4096,512]{1,0:T(8,128)(2,1)S(1)} %get-tuple-element.84.refs_1_.refs_2_, f32[1552,128]{1,0:T(8,128)S(1)} %collective-permute-done.22.refs_3_, ...), custom_call_target="tpu_custom_call" | custom-call | flops 2415919104 | bytes 1572864 | tf_op jit(solution)/shard_map/pallas_call | solution.py:175
  (61 shorter events, 0.3 us)
Async XLA Ops:
  6.5 57.0 %all-gather.2.cloned.1.call-start = ((), (), s32[]{:S(2)}) async-start(), calls=%async_computation | async-start | bytes 9437184 | tf_op jit(solution)/shard_map/all_gather | solution.py:196
  6.5 0.7 copy-start.14
  7.2 0.7 copy-start.15
  11.0 22.6 %copy-start.18 = (f32[1032,128]{1,0:T(8,128)}, f32[1032,128]{1,0:T(8,128)S(1)}, u32[]{:S(2)}) copy-start(f32[1032,128]{1,0:T(8,128)S(1)} %get-tuple-element.54.refs_3_) | copy-start | bytes 1585156
  11.0 31.1 %copy-start.16 = (f32[1032,128]{1,0:T(8,128)}, f32[1032,128]{1,0:T(8,128)S(1)}, u32[]{:S(2)}) copy-start(f32[1032,128]{1,0:T(8,128)S(1)} %get-tuple-element.53.refs_2_) | copy-start | bytes 1585156
  11.0 10.5 %collective-permute-start = (f32[1032,128]{1,0:T(8,128)S(1)}, f32[1032,128]{1,0:T(8,128)S(1)}, u32[]{:S(2)}, u32[]{:S(2)}) collective-permute-start(f32[1032,128]{1,0:T(8,128)S(1)} %get-tuple-element.53.refs_2_), channel_id=1, source_target_pairs={{0,1},{1,2},{2,3},{3,0},{16,19},{17,16},{18,17},{19,18},{4,5},{5,6... | collective-permute-start | bytes 1585160 | tf_op jit(solution)/shard_map/ppermute | solution.py:25
  12.6 10.4 %collective-permute-start.1 = (f32[1032,128]{1,0:T(8,128)S(1)}, f32[1032,128]{1,0:T(8,128)S(1)}, u32[]{:S(2)}, u32[]{:S(2)}) collective-permute-start(f32[1032,128]{1,0:T(8,128)S(1)} %get-tuple-element.54.refs_3_), channel_id=1, source_target_pairs={{0,4},{4,8},{8,12},{12,0},{16,28},{20,16},{24,20},{28,24},{1,5},{5... | collective-permute-start | bytes 1585160 | tf_op jit(solution)/shard_map/ppermute | solution.py:25
  14.2 14.5 %collective-permute-start.5 = (f32[1032,128]{1,0:T(8,128)S(1)}, f32[1032,128]{1,0:T(8,128)S(1)}, u32[]{:S(2)}, u32[]{:S(2)}) collective-permute-start(f32[1032,128]{1,0:T(8,128)S(1)} %get-tuple-element.53.refs_2_), channel_id=1, source_target_pairs={{0,4},{4,8},{8,12},{12,0},{16,28},{20,16},{24,20},{28,24},{1,5},{5... | collective-permute-start | bytes 1585160 | tf_op jit(solution)/shard_map/ppermute | solution.py:25
  15.8 12.9 %collective-permute-start.4 = (f32[1032,128]{1,0:T(8,128)S(1)}, f32[1032,128]{1,0:T(8,128)S(1)}, u32[]{:S(2)}, u32[]{:S(2)}) collective-permute-start(f32[1032,128]{1,0:T(8,128)S(1)} %get-tuple-element.54.refs_3_), channel_id=1, source_target_pairs={{0,1},{1,2},{2,3},{3,0},{16,19},{17,16},{18,17},{19,18},{4,5},{5,6... | collective-permute-start | bytes 1585160 | tf_op jit(solution)/shard_map/ppermute | solution.py:25
  23.1 11.9 %copy-start = (f32[1032,128]{1,0:T(8,128)}, f32[1032,128]{1,0:T(8,128)S(1)}, u32[]{:S(2)}) copy-start(f32[1032,128]{1,0:T(8,128)S(1)} %collective-permute-done.1.refs_5_) | copy-start | bytes 1585156
  23.1 10.4 %collective-permute-start.2 = (f32[1032,128]{1,0:T(8,128)S(1)}, f32[1032,128]{1,0:T(8,128)S(1)}, u32[]{:S(2)}, u32[]{:S(2)}) collective-permute-start(f32[1032,128]{1,0:T(8,128)S(1)} %collective-permute-done.refs_4_), channel_id=1, source_target_pairs={{0,1},{1,2},{2,3},{3,0},{16,19},{17,16},{18,17},{19,18},{4,5},{5,6... | collective-permute-start | bytes 1585160 | tf_op jit(solution)/shard_map/ppermute | solution.py:25
  24.6 10.4 %collective-permute-start.3 = (f32[1032,128]{1,0:T(8,128)S(1)}, f32[1032,128]{1,0:T(8,128)S(1)}, u32[]{:S(2)}, u32[]{:S(2)}) collective-permute-start(f32[1032,128]{1,0:T(8,128)S(1)} %collective-permute-done.1.refs_5_), channel_id=1, source_target_pairs={{0,4},{4,8},{8,12},{12,0},{16,28},{20,16},{24,20},{28,24},{1,5},{5... | collective-permute-start | bytes 1585160 | tf_op jit(solution)/shard_map/ppermute | solution.py:25
  28.7 10.5 %copy-start.20 = (f32[1032,128]{1,0:T(8,128)}, f32[1032,128]{1,0:T(8,128)S(1)}, u32[]{:S(2)}) copy-start(f32[1032,128]{1,0:T(8,128)S(1)} %collective-permute-done.5.refs_7_) | copy-start | bytes 1585156
  28.8 12.0 %copy-start.22 = (f32[1032,128]{1,0:T(8,128)}, f32[1032,128]{1,0:T(8,128)S(1)}, u32[]{:S(2)}) copy-start(f32[1032,128]{1,0:T(8,128)S(1)} %collective-permute-done.4.refs_6_) | copy-start | bytes 1585156
  28.8 10.5 %collective-permute-start.8 = (f32[1032,128]{1,0:T(8,128)S(1)}, f32[1032,128]{1,0:T(8,128)S(1)}, u32[]{:S(2)}, u32[]{:S(2)}) collective-permute-start(f32[1032,128]{1,0:T(8,128)S(1)} %collective-permute-done.4.refs_6_), channel_id=1, source_target_pairs={{0,1},{1,2},{2,3},{3,0},{16,19},{17,16},{18,17},{19,18},{4,5},{5,6... | collective-permute-start | bytes 1585160 | tf_op jit(solution)/shard_map/ppermute | solution.py:25
  30.3 10.4 %collective-permute-start.9 = (f32[1032,128]{1,0:T(8,128)S(1)}, f32[1032,128]{1,0:T(8,128)S(1)}, u32[]{:S(2)}, u32[]{:S(2)}) collective-permute-start(f32[1032,128]{1,0:T(8,128)S(1)} %collective-permute-done.5.refs_7_), channel_id=1, source_target_pairs={{0,4},{4,8},{8,12},{12,0},{16,28},{20,16},{24,20},{28,24},{1,5},{5... | collective-permute-start | bytes 1585160 | tf_op jit(solution)/shard_map/ppermute | solution.py:25
  33.5 11.9 %copy-start.2 = (f32[1032,128]{1,0:T(8,128)}, f32[1032,128]{1,0:T(8,128)S(1)}, u32[]{:S(2)}) copy-start(f32[1032,128]{1,0:T(8,128)S(1)} %collective-permute-done.2.refs_8_) | copy-start | bytes 1585156
  35.0 10.4 %copy-start.4 = (f32[1032,128]{1,0:T(8,128)}, f32[1032,128]{1,0:T(8,128)S(1)}, u32[]{:S(2)}) copy-start(f32[1032,128]{1,0:T(8,128)S(1)} %collective-permute-done.3.refs_9_) | copy-start | bytes 1585156
  35.0 10.4 %collective-permute-start.6 = (f32[1032,128]{1,0:T(8,128)S(1)}, f32[1032,128]{1,0:T(8,128)S(1)}, u32[]{:S(2)}, u32[]{:S(2)}) collective-permute-start(f32[1032,128]{1,0:T(8,128)S(1)} %collective-permute-done.2.refs_8_), channel_id=1, source_target_pairs={{0,1},{1,2},{2,3},{3,0},{16,19},{17,16},{18,17},{19,18},{4,5},{5,6... | collective-permute-start | bytes 1585160 | tf_op jit(solution)/shard_map/ppermute | solution.py:25
  36.2 10.4 %collective-permute-start.7 = (f32[1032,128]{1,0:T(8,128)S(1)}, f32[1032,128]{1,0:T(8,128)S(1)}, u32[]{:S(2)}, u32[]{:S(2)}) collective-permute-start(f32[1032,128]{1,0:T(8,128)S(1)} %collective-permute-done.3.refs_9_), channel_id=1, source_target_pairs={{0,4},{4,8},{8,12},{12,0},{16,28},{20,16},{24,20},{28,24},{1,5},{5... | collective-permute-start | bytes 1585160 | tf_op jit(solution)/shard_map/ppermute | solution.py:25
  39.3 15.1 %copy-start.6 = (f32[1032,128]{1,0:T(8,128)}, f32[1032,128]{1,0:T(8,128)S(1)}, u32[]{:S(2)}) copy-start(f32[1032,128]{1,0:T(8,128)S(1)} %collective-permute-done.8.refs_3_) | copy-start | bytes 1585156
  40.7 13.6 %copy-start.8 = (f32[1032,128]{1,0:T(8,128)}, f32[1032,128]{1,0:T(8,128)S(1)}, u32[]{:S(2)}) copy-start(f32[1032,128]{1,0:T(8,128)S(1)} %collective-permute-done.9.refs_4_) | copy-start | bytes 1585156
  40.8 10.4 %collective-permute-start.12 = (f32[1032,128]{1,0:T(8,128)S(1)}, f32[1032,128]{1,0:T(8,128)S(1)}, u32[]{:S(2)}, u32[]{:S(2)}) collective-permute-start(f32[1032,128]{1,0:T(8,128)S(1)} %collective-permute-done.8.refs_3_), channel_id=1, source_target_pairs={{0,1},{1,2},{2,3},{3,0},{16,19},{17,16},{18,17},{19,18},{4,5},{5,6... | collective-permute-start | bytes 1585160 | tf_op jit(solution)/shard_map/ppermute | solution.py:25
  41.9 10.4 %collective-permute-start.13 = (f32[1032,128]{1,0:T(8,128)S(1)}, f32[1032,128]{1,0:T(8,128)S(1)}, u32[]{:S(2)}, u32[]{:S(2)}) collective-permute-start(f32[1032,128]{1,0:T(8,128)S(1)} %collective-permute-done.9.refs_4_), channel_id=1, source_target_pairs={{0,4},{4,8},{8,12},{12,0},{16,28},{20,16},{24,20},{28,24},{1,5},{5... | collective-permute-start | bytes 1585160 | tf_op jit(solution)/shard_map/ppermute | solution.py:25
  46.7 13.3 %collective-permute-start.10 = (f32[1552,128]{1,0:T(8,128)S(1)}, f32[1552,128]{1,0:T(8,128)S(1)}, u32[]{:S(2)}, u32[]{:S(2)}) collective-permute-start(f32[1552,128]{1,0:T(8,128)S(1)} %pad_maximum_fusion), channel_id=1, source_target_pairs={{0,1},{1,2},{2,3},{3,0},{16,19},{17,16},{18,17},{19,18},{4,5},{5,6... | collective-permute-start | bytes 2383880 | tf_op jit(solution)/shard_map/ppermute | solution.py:25
  47.6 13.3 %collective-permute-start.11 = (f32[1552,128]{1,0:T(8,128)S(1)}, f32[1552,128]{1,0:T(8,128)S(1)}, u32[]{:S(2)}, u32[]{:S(2)}) collective-permute-start(f32[1552,128]{1,0:T(8,128)S(1)} %pad_maximum_fusion.1), channel_id=1, source_target_pairs={{0,4},{4,8},{8,12},{12,0},{16,28},{20,16},{24,20},{28,24},{1,5},{5... | collective-permute-start | bytes 2383880 | tf_op jit(solution)/shard_map/ppermute | solution.py:25
  51.2 8.8 %copy-start.10 = (f32[1032,128]{1,0:T(8,128)}, f32[1032,128]{1,0:T(8,128)S(1)}, u32[]{:S(2)}) copy-start(f32[1032,128]{1,0:T(8,128)S(1)} %collective-permute-done.12.refs_7_) | copy-start | bytes 1585156
  52.4 7.6 %copy-start.12 = (f32[1032,128]{1,0:T(8,128)}, f32[1032,128]{1,0:T(8,128)S(1)}, u32[]{:S(2)}) copy-start(f32[1032,128]{1,0:T(8,128)S(1)} %collective-permute-done.13.refs_8_) | copy-start | bytes 1585156
  63.6 3.8 %copy-start.24 = (f32[1552,128]{1,0:T(8,128)S(1)}, f32[1552,128]{1,0:T(8,128)}, u32[]{:S(2)}) copy-start(f32[1552,128]{1,0:T(8,128)} %pad_maximum_fusion.2) | copy-start | bytes 2383876
  63.6 5.4 %copy-start.25 = (f32[1552,128]{1,0:T(8,128)S(1)}, f32[1552,128]{1,0:T(8,128)}, u32[]{:S(2)}) copy-start(f32[1552,128]{1,0:T(8,128)} %pad_maximum_fusion.3) | copy-start | bytes 2383876
  63.6 20.4 %copy-start.1 = (f32[1032,128]{1,0:T(8,128)S(1)}, f32[1032,128]{1,0:T(8,128)}, u32[]{:S(2)}) copy-start(f32[1032,128]{1,0:T(8,128)} %copy-done) | copy-start | bytes 1585156
  63.6 20.4 %copy-start.3 = (f32[1032,128]{1,0:T(8,128)S(1)}, f32[1032,128]{1,0:T(8,128)}, u32[]{:S(2)}) copy-start(f32[1032,128]{1,0:T(8,128)} %copy-done.2) | copy-start | bytes 1585156
  63.6 20.4 %copy-start.5 = (f32[1032,128]{1,0:T(8,128)S(1)}, f32[1032,128]{1,0:T(8,128)}, u32[]{:S(2)}) copy-start(f32[1032,128]{1,0:T(8,128)} %copy-done.4) | copy-start | bytes 1585156
  63.6 20.4 %copy-start.17 = (f32[1032,128]{1,0:T(8,128)S(1)}, f32[1032,128]{1,0:T(8,128)}, u32[]{:S(2)}) copy-start(f32[1032,128]{1,0:T(8,128)} %copy-done.16) | copy-start | bytes 1585156
  63.6 20.4 %copy-start.19 = (f32[1032,128]{1,0:T(8,128)S(1)}, f32[1032,128]{1,0:T(8,128)}, u32[]{:S(2)}) copy-start(f32[1032,128]{1,0:T(8,128)} %copy-done.18) | copy-start | bytes 1585156
  63.6 20.4 %copy-start.21 = (f32[1032,128]{1,0:T(8,128)S(1)}, f32[1032,128]{1,0:T(8,128)}, u32[]{:S(2)}) copy-start(f32[1032,128]{1,0:T(8,128)} %copy-done.20) | copy-start | bytes 1585156
  63.6 20.4 %copy-start.23 = (f32[1032,128]{1,0:T(8,128)S(1)}, f32[1032,128]{1,0:T(8,128)}, u32[]{:S(2)}) copy-start(f32[1032,128]{1,0:T(8,128)} %copy-done.22) | copy-start | bytes 1585156
  67.4 25.4 %copy-start.7 = (f32[1032,128]{1,0:T(8,128)S(1)}, f32[1032,128]{1,0:T(8,128)}, u32[]{:S(2)}) copy-start(f32[1032,128]{1,0:T(8,128)} %copy-done.6) | copy-start | bytes 1585156
  67.4 25.4 %copy-start.9 = (f32[1032,128]{1,0:T(8,128)S(1)}, f32[1032,128]{1,0:T(8,128)}, u32[]{:S(2)}) copy-start(f32[1032,128]{1,0:T(8,128)} %copy-done.8) | copy-start | bytes 1585156
  67.4 25.3 %copy-start.11 = (f32[1032,128]{1,0:T(8,128)S(1)}, f32[1032,128]{1,0:T(8,128)}, u32[]{:S(2)}) copy-start(f32[1032,128]{1,0:T(8,128)} %copy-done.10) | copy-start | bytes 1585156
  67.4 25.3 %copy-start.13 = (f32[1032,128]{1,0:T(8,128)S(1)}, f32[1032,128]{1,0:T(8,128)}, u32[]{:S(2)}) copy-start(f32[1032,128]{1,0:T(8,128)} %copy-done.12) | copy-start | bytes 1585156
  67.4 13.4 %collective-permute-start.14 = (f32[1552,128]{1,0:T(8,128)S(1)}, f32[1552,128]{1,0:T(8,128)S(1)}, u32[]{:S(2)}, u32[]{:S(2)}) collective-permute-start(f32[1552,128]{1,0:T(8,128)S(1)} %copy-done.24), channel_id=1, source_target_pairs={{0,1},{1,2},{2,3},{3,0},{16,19},{17,16},{18,17},{19,18},{4,5},{5,6... | collective-permute-start | bytes 2383880 | tf_op jit(solution)/shard_map/ppermute | solution.py:25
  69.0 13.3 %collective-permute-start.15 = (f32[1552,128]{1,0:T(8,128)S(1)}, f32[1552,128]{1,0:T(8,128)S(1)}, u32[]{:S(2)}, u32[]{:S(2)}) collective-permute-start(f32[1552,128]{1,0:T(8,128)S(1)} %copy-done.25), channel_id=1, source_target_pairs={{0,4},{4,8},{8,12},{12,0},{16,28},{20,16},{24,20},{28,24},{1,5},{5... | collective-permute-start | bytes 2383880 | tf_op jit(solution)/shard_map/ppermute | solution.py:25
  70.5 19.5 %collective-permute-start.16 = (f32[1552,128]{1,0:T(8,128)S(1)}, f32[1552,128]{1,0:T(8,128)S(1)}, u32[]{:S(2)}, u32[]{:S(2)}) collective-permute-start(f32[1552,128]{1,0:T(8,128)S(1)} %collective-permute-done.10.refs_3_), channel_id=1, source_target_pairs={{0,1},{1,2},{2,3},{3,0},{16,19},{17,16},{18,17},{19,18},{4,5},{5,6... | collective-permute-start | bytes 2383880 | tf_op jit(solution)/shard_map/ppermute | solution.py:25
  71.9 18.8 %collective-permute-start.17 = (f32[1552,128]{1,0:T(8,128)S(1)}, f32[1552,128]{1,0:T(8,128)S(1)}, u32[]{:S(2)}, u32[]{:S(2)}) collective-permute-start(f32[1552,128]{1,0:T(8,128)S(1)} %collective-permute-done.11.refs_4_), channel_id=1, source_target_pairs={{0,4},{4,8},{8,12},{12,0},{16,28},{20,16},{24,20},{28,24},{1,5},{5... | collective-permute-start | bytes 2383880 | tf_op jit(solution)/shard_map/ppermute | solution.py:25
  82.3 15.6 %collective-permute-start.18 = (f32[1552,128]{1,0:T(8,128)S(1)}, f32[1552,128]{1,0:T(8,128)S(1)}, u32[]{:S(2)}, u32[]{:S(2)}) collective-permute-start(f32[1552,128]{1,0:T(8,128)S(1)} %collective-permute-done.14.refs_5_), channel_id=1, source_target_pairs={{0,1},{1,2},{2,3},{3,0},{16,19},{17,16},{18,17},{19,18},{4,5},{5,6... | collective-permute-start | bytes 2383880 | tf_op jit(solution)/shard_map/ppermute | solution.py:25
  83.7 15.6 %collective-permute-start.19 = (f32[1552,128]{1,0:T(8,128)S(1)}, f32[1552,128]{1,0:T(8,128)S(1)}, u32[]{:S(2)}, u32[]{:S(2)}) collective-permute-start(f32[1552,128]{1,0:T(8,128)S(1)} %collective-permute-done.15.refs_6_), channel_id=1, source_target_pairs={{0,4},{4,8},{8,12},{12,0},{16,28},{20,16},{24,20},{28,24},{1,5},{5... | collective-permute-start | bytes 2383880 | tf_op jit(solution)/shard_map/ppermute | solution.py:25
  90.8 15.6 %collective-permute-start.20 = (f32[1552,128]{1,0:T(8,128)S(1)}, f32[1552,128]{1,0:T(8,128)S(1)}, u32[]{:S(2)}, u32[]{:S(2)}) collective-permute-start(f32[1552,128]{1,0:T(8,128)S(1)} %collective-permute-done.16.refs_3_), channel_id=1, source_target_pairs={{0,1},{1,2},{2,3},{3,0},{16,19},{17,16},{18,17},{19,18},{4,5},{5,6... | collective-permute-start | bytes 2383880 | tf_op jit(solution)/shard_map/ppermute | solution.py:25
  92.2 15.6 %collective-permute-start.21 = (f32[1552,128]{1,0:T(8,128)S(1)}, f32[1552,128]{1,0:T(8,128)S(1)}, u32[]{:S(2)}, u32[]{:S(2)}) collective-permute-start(f32[1552,128]{1,0:T(8,128)S(1)} %collective-permute-done.17.refs_4_), channel_id=1, source_target_pairs={{0,4},{4,8},{8,12},{12,0},{16,28},{20,16},{24,20},{28,24},{1,5},{5... | collective-permute-start | bytes 2383880 | tf_op jit(solution)/shard_map/ppermute | solution.py:25
  99.3 15.6 %collective-permute-start.22 = (f32[1552,128]{1,0:T(8,128)S(1)}, f32[1552,128]{1,0:T(8,128)S(1)}, u32[]{:S(2)}, u32[]{:S(2)}) collective-permute-start(f32[1552,128]{1,0:T(8,128)S(1)} %collective-permute-done.18.refs_5_), channel_id=1, source_target_pairs={{0,1},{1,2},{2,3},{3,0},{16,19},{17,16},{18,17},{19,18},{4,5},{5,6... | collective-permute-start | bytes 2383880 | tf_op jit(solution)/shard_map/ppermute | solution.py:25
  100.8 15.6 %collective-permute-start.23 = (f32[1552,128]{1,0:T(8,128)S(1)}, f32[1552,128]{1,0:T(8,128)S(1)}, u32[]{:S(2)}, u32[]{:S(2)}) collective-permute-start(f32[1552,128]{1,0:T(8,128)S(1)} %collective-permute-done.19.refs_6_), channel_id=1, source_target_pairs={{0,4},{4,8},{8,12},{12,0},{16,28},{20,16},{24,20},{28,24},{1,5},{5... | collective-permute-start | bytes 2383880 | tf_op jit(solution)/shard_map/ppermute | solution.py:25
Sparse Core Ops, SparseCore 0:
  11.1 52.3 all-gather.1

commit v3 on v2

--- a/solution.py
+++ b/solution.py
@@ -29,13 +29,36 @@
     return lax.optimization_barrier((ring(pair[0], "x", NX), ring(pair[1], "y", NY)))
 
 
-def prepare_kernel(index, mask, tiles_ref, d_ref, a_ref, b_ref, masked_ref, d_buf, sem):
+def mask_kernel(mask, d_ref, masked_ref, d_buf, sem):
+    size = d_ref.shape[0] // mask.shape[0]
+    rows = [pl.ds(i * size, size) for i in range(mask.shape[0])]
+    copies = [pltpu.make_async_copy(d_ref.at[r, :], d_buf.at[r, :], sem.at[i]) for i, r in enumerate(rows)]
+    for c in copies:
+        c.start()
+    for i, c in enumerate(copies):
+        c.wait()
+        for j in range(mask.shape[1]):
+            block = slice(i * size, (i + 1) * size), slice(j * size, (j + 1) * size)
+            masked_ref[block] = d_buf[block] * mask[i, j].astype(jnp.float32)
+
+
+def mask_blocks(mask, d):
+    return pl.pallas_call(
+        mask_kernel,
+        in_specs=[pl.BlockSpec(memory_space=pltpu.SMEM), pl.BlockSpec(memory_space=pltpu.HBM)],
+        out_specs=pl.BlockSpec(memory_space=pltpu.VMEM),
+        out_shape=pltpu.VMEM(d.shape, jnp.float32),
+        scratch_shapes=[pltpu.VMEM(d.shape, jnp.float32), pltpu.SemaphoreType.DMA((mask.shape[0],))],
+        compiler_params=pltpu.CompilerParams(vmem_limit_bytes=8 * MIB),
+        cost_estimate=pl.CostEstimate(flops=d.size, bytes_accessed=8 * d.size, transcendentals=0),
+    )(mask, pltpu.with_memory_space_constraint(d, pltpu.HBM))
+
+
+def payload_kernel(index, tiles_ref, a_ref, b_ref, sem):
     data = HALF * a_ref.shape[1]
-    size = d_ref.shape[0] // mask.shape[0]
     copies = [
-        pltpu.make_async_copy(d_ref, d_buf, sem.at[0]),
-        pltpu.make_async_copy(tiles_ref.at[pl.ds(0, data), :], a_ref.at[pl.ds(0, data), :], sem.at[1]),
-        pltpu.make_async_copy(tiles_ref.at[pl.ds(data, data), :], b_ref.at[pl.ds(0, data), :], sem.at[2]),
+        pltpu.make_async_copy(tiles_ref.at[pl.ds(0, data), :], a_ref.at[pl.ds(0, data), :], sem.at[0]),
+        pltpu.make_async_copy(tiles_ref.at[pl.ds(data, data), :], b_ref.at[pl.ds(0, data), :], sem.at[1]),
     ]
     for c in copies:
         c.start()
@@ -45,30 +68,22 @@
         for j in range(HALF):
             places = jnp.where(lane == j, index[n * HALF + j], places)
         ref[data:, :] = places.astype(jnp.float32)
-    copies[0].wait()
-    for i in range(mask.shape[0]):
-        for j in range(mask.shape[1]):
-            block = slice(i * size, (i + 1) * size), slice(j * size, (j + 1) * size)
-            masked_ref[block] = d_buf[block] * mask[i, j].astype(jnp.float32)
-    copies[1].wait()
-    copies[2].wait()
-
-
-def prepare(a_tiles, index, d, mask):
+    for c in copies:
+        c.wait()
+
+
+def payloads(a_tiles, index):
     stored, size = a_tiles.shape[0], a_tiles.shape[1]
-    smem = pl.BlockSpec(memory_space=pltpu.SMEM)
-    vmem = pl.BlockSpec(memory_space=pltpu.VMEM)
     payload = pltpu.VMEM((HALF * size + MARK, size), jnp.float32)
-    hbm = [pltpu.with_memory_space_constraint(v, pltpu.HBM) for v in (a_tiles.reshape(stored * size, size), d)]
-    return pl.pallas_call(
-        prepare_kernel,
-        in_specs=[smem, smem] + [pl.BlockSpec(memory_space=pltpu.HBM)] * 2,
-        out_specs=[vmem] * 3,
-        out_shape=[payload, payload, pltpu.VMEM(d.shape, jnp.float32)],
-        scratch_shapes=[pltpu.VMEM(d.shape, jnp.float32), pltpu.SemaphoreType.DMA((3,))],
+    return pl.pallas_call(
+        payload_kernel,
+        in_specs=[pl.BlockSpec(memory_space=pltpu.SMEM), pl.BlockSpec(memory_space=pltpu.HBM)],
+        out_specs=[pl.BlockSpec(memory_space=pltpu.VMEM)] * 2,
+        out_shape=[payload, payload],
+        scratch_shapes=[pltpu.SemaphoreType.DMA((2,))],
         compiler_params=pltpu.CompilerParams(vmem_limit_bytes=8 * MIB),
-        cost_estimate=pl.CostEstimate(flops=d.size, bytes_accessed=16 * d.size, transcendentals=0),
-    )(index, mask, *hbm)
+        cost_estimate=pl.CostEstimate(flops=0, bytes_accessed=8 * a_tiles.size, transcendentals=0),
+    )(index, pltpu.with_memory_space_constraint(a_tiles.reshape(stored * size, size), pltpu.HBM))
 
 
 def after(pair, others):
@@ -192,8 +207,8 @@
     stored, size = a_tiles.shape[0], a_tiles.shape[1]
     few = HALF // 2
     data = HALF * size
-    a, b, masked = prepare(a_tiles, a_index, d_values, d_mask)
-    density = lax.all_gather(masked, ("z", "core"), axis=0, tiled=True)
+    density = lax.all_gather(mask_blocks(d_mask, d_values), ("z", "core"), axis=0, tiled=True)
+    a, b = payloads(a_tiles, a_index)
 
     whole = [(0, j) for j in range(HALF)]
 

time: 128 us -> 127 us (level)
  waiting for transfers between devices: 50.9 us -> 46.9 us
  local copies, waits for them, and re-layouts: 1.68 us -> 3.27 us
  Pallas kernels: 34.7 us -> 36.2 us
    all_gather x1, waiting for transfers between devices: 2.66 us -> 0.24 us  [body(): lax.all_gather(mask_blocks(d_mask, d_values), ('z', 'core'), axis=0, tile...]
    ppermute x24, waiting for transfers between devices: 48.2 us -> 46.6 us  [ring(): lax.ppermute(v, ('z', 'core') if axis == 'z' else ('core', axis), perm)]
    unnamed x52, local copies, waits for them, and re-layouts: 1.43 us -> 3.02 us
    pallas_call x1 -> x2, Pallas kernels: 3.08 us -> 4.54 us  [the longest x1 2.79 us: mask_blocks(): pl.pallas_call(mask_kernel, in_specs=[pl.BlockSpec(memory_space=pltpu.SME...]
  transfers between devices with their start and end apart: 25 -> 25, of which waited for: 21 -> 21; matrix products, arithmetic and copies ran while one was open for 2% -> 2% of each run, Pallas kernels for 18% -> 20%
where the time goes in v3:
time: 127 us
  waiting for transfers between devices  46.9 us (37%)
  Pallas kernels  36.2 us (29%)
  starting transfers between devices  24.9 us (20%)
  between operations  13.7 us (11%)
  local copies, waits for them, and re-layouts  3.27 us (3%)
  other arithmetic  2.1 us (2%)
    ppermute x24, waiting for transfers between devices, ring(): lax.ppermute(v, ('z', 'core') if axis == 'z' else ('core', axis), perm)  46.6 us
    pallas_call x5, Pallas kernels, add_products(): pl.pallas_call(functools.partial(add_kernel, marks, first, last, size), i...  27.9 us
    ppermute x24, starting transfers between devices, ring(): lax.ppermute(v, ('z', 'core') if axis == 'z' else ('core', axis), perm)  24.9 us
    pallas_call x1, Pallas kernels, split(): pl.pallas_call(split_kernel, in_specs=[pl.BlockSpec(memory_space=pltpu.HB...  3.76 us
    unnamed x52, local copies, waits for them, and re-layouts  3.02 us
    pallas_call x1, Pallas kernels, mask_blocks(): pl.pallas_call(mask_kernel, in_specs=[pl.BlockSpec(memory_space=pltpu.SME...  2.79 us
  transfers between devices with their start and end apart: 25, of which 21 were waited for; matrix products, arithmetic and copies ran while one was open for 2% of the time, Pallas kernels for 20%

profile of v3, /device:TPU:0, one launch (start us, length us, event | category | flops | bytes accessed | tf_op | source)
XLA Modules:
  0.0 127.0 jit_solution(4799155934298597160)
XLA Ops:
  6.5 0.7 copy-done.14
  7.2 2.8 %shard_map.47 = f32[512,512]{1,0:T(8,128)} custom-call(s32[4,4]{1,0:T(4,128)S(1)} %copy-done.14, f32[512,512]{1,0:T(8,128)} %d_ref.1), custom_call_target="tpu_custom_call" | custom-call | flops 262144 | bytes 2097152 | tf_op jit(solution)/shard_map/pallas_call | solution.py:46
  10.0 0.0 all-gather.2.cloned.1.call-update
  10.0 0.0 copy-start.15
  10.1 0.6 copy-done.15
  10.7 1.8 %shard_map.46 = (f32[1032,128]{1,0:T(8,128)S(1)}, f32[1032,128]{1,0:T(8,128)S(1)}) custom-call(s32[16]{0:T(128)S(1)} %copy-done.15, f32[2048,128]{1,0:T(8,128)} %bitcast.1), custom_call_target="tpu_custom_call" | custom-call | bytes 2097152 | tf_op jit(solution)/shard_map/pallas_call | solution.py:78
  12.5 1.6 %collective-permute-start = (f32[1032,128]{1,0:T(8,128)S(1)}, f32[1032,128]{1,0:T(8,128)S(1)}, u32[]{:S(2)}, u32[]{:S(2)}) collective-permute-start(f32[1032,128]{1,0:T(8,128)S(1)} %get-tuple-element.52.refs_2_), channel_id=1, source_target_pairs={{0,1},{1,2},{2,3},{3,0},{16,19},{17,16},{18,17},{19,18},{4,5},{5,6... | collective-permute-start | bytes 1585160 | tf_op jit(solution)/shard_map/ppermute | solution.py:25
  14.1 1.6 %collective-permute-start.1 = (f32[1032,128]{1,0:T(8,128)S(1)}, f32[1032,128]{1,0:T(8,128)S(1)}, u32[]{:S(2)}, u32[]{:S(2)}) collective-permute-start(f32[1032,128]{1,0:T(8,128)S(1)} %get-tuple-element.53.refs_3_), channel_id=1, source_target_pairs={{0,4},{4,8},{8,12},{12,0},{16,28},{20,16},{24,20},{28,24},{1,5},{5... | collective-permute-start | bytes 1585160 | tf_op jit(solution)/shard_map/ppermute | solution.py:25
  15.7 1.6 %collective-permute-start.5 = (f32[1032,128]{1,0:T(8,128)S(1)}, f32[1032,128]{1,0:T(8,128)S(1)}, u32[]{:S(2)}, u32[]{:S(2)}) collective-permute-start(f32[1032,128]{1,0:T(8,128)S(1)} %get-tuple-element.52.refs_2_), channel_id=1, source_target_pairs={{0,4},{4,8},{8,12},{12,0},{16,28},{20,16},{24,20},{28,24},{1,5},{5... | collective-permute-start | bytes 1585160 | tf_op jit(solution)/shard_map/ppermute | solution.py:25
  17.3 0.8 copy-done.16
  18.1 1.5 %collective-permute-start.4 = (f32[1032,128]{1,0:T(8,128)S(1)}, f32[1032,128]{1,0:T(8,128)S(1)}, u32[]{:S(2)}, u32[]{:S(2)}) collective-permute-start(f32[1032,128]{1,0:T(8,128)S(1)} %get-tuple-element.53.refs_3_), channel_id=1, source_target_pairs={{0,1},{1,2},{2,3},{3,0},{16,19},{17,16},{18,17},{19,18},{4,5},{5,6... | collective-permute-start | bytes 1585160 | tf_op jit(solution)/shard_map/ppermute | solution.py:25
  19.6 0.8 copy-done.18
  20.4 2.6 %collective-permute-done.refs_4_ = f32[1032,128]{1,0:T(8,128)S(1)} collective-permute-done((f32[1032,128]{1,0:T(8,128)S(1)}, f32[1032,128]{1,0:T(8,128)S(1)}, u32[]{:S(2)}, u32[]{:S(2)}) %collective-permute-start) | collective-permute-done | bytes 528416 | tf_op jit(solution)/shard_map/ppermute | solution.py:25
  23.0 1.6 %collective-permute-done.1.refs_5_ = f32[1032,128]{1,0:T(8,128)S(1)} collective-permute-done((f32[1032,128]{1,0:T(8,128)S(1)}, f32[1032,128]{1,0:T(8,128)S(1)}, u32[]{:S(2)}, u32[]{:S(2)}) %collective-permute-start.1) | collective-permute-done | bytes 528416 | tf_op jit(solution)/shard_map/ppermute | solution.py:25
  24.5 1.5 %collective-permute-start.2 = (f32[1032,128]{1,0:T(8,128)S(1)}, f32[1032,128]{1,0:T(8,128)S(1)}, u32[]{:S(2)}, u32[]{:S(2)}) collective-permute-start(f32[1032,128]{1,0:T(8,128)S(1)} %collective-permute-done.refs_4_), channel_id=1, source_target_pairs={{0,1},{1,2},{2,3},{3,0},{16,19},{17,16},{18,17},{19,18},{4,5},{5,6... | collective-permute-start | bytes 1585160 | tf_op jit(solution)/shard_map/ppermute | solution.py:25
  26.0 0.4 collective-permute-start.3
  26.4 3.8 %collective-permute-done.5.refs_7_ = f32[1032,128]{1,0:T(8,128)S(1)} collective-permute-done((f32[1032,128]{1,0:T(8,128)S(1)}, f32[1032,128]{1,0:T(8,128)S(1)}, u32[]{:S(2)}, u32[]{:S(2)}) %collective-permute-start.5) | collective-permute-done | bytes 528416 | tf_op jit(solution)/shard_map/ppermute | solution.py:25
  30.2 1.6 %collective-permute-start.8 = (f32[1032,128]{1,0:T(8,128)S(1)}, f32[1032,128]{1,0:T(8,128)S(1)}, u32[]{:S(2)}, u32[]{:S(2)}) collective-permute-start(f32[1032,128]{1,0:T(8,128)S(1)} %collective-permute-done.4.refs_6_), channel_id=1, source_target_pairs={{0,1},{1,2},{2,3},{3,0},{16,19},{17,16},{18,17},{19,18},{4,5},{5,6... | collective-permute-start | bytes 1585160 | tf_op jit(solution)/shard_map/ppermute | solution.py:25
  31.8 0.4 collective-permute-start.9
  32.2 2.8 %collective-permute-done.2.refs_8_ = f32[1032,128]{1,0:T(8,128)S(1)} collective-permute-done((f32[1032,128]{1,0:T(8,128)S(1)}, f32[1032,128]{1,0:T(8,128)S(1)}, u32[]{:S(2)}, u32[]{:S(2)}) %collective-permute-start.2) | collective-permute-done | bytes 528416 | tf_op jit(solution)/shard_map/ppermute | solution.py:25
  35.0 1.5 %collective-permute-done.3.refs_9_ = f32[1032,128]{1,0:T(8,128)S(1)} collective-permute-done((f32[1032,128]{1,0:T(8,128)S(1)}, f32[1032,128]{1,0:T(8,128)S(1)}, u32[]{:S(2)}, u32[]{:S(2)}) %collective-permute-start.3) | collective-permute-done | bytes 528416 | tf_op jit(solution)/shard_map/ppermute | solution.py:25
  36.5 1.2 collective-permute-start.6
  37.7 0.1 collective-permute-start.7
  37.7 0.1 fusion
  37.8 2.9 %collective-permute-done.8.refs_3_ = f32[1032,128]{1,0:T(8,128)S(1)} collective-permute-done((f32[1032,128]{1,0:T(8,128)S(1)}, f32[1032,128]{1,0:T(8,128)S(1)}, u32[]{:S(2)}, u32[]{:S(2)}) %collective-permute-start.8) | collective-permute-done | bytes 528416 | tf_op jit(solution)/shard_map/ppermute | solution.py:25
  40.7 1.5 %collective-permute-done.9.refs_4_ = f32[1032,128]{1,0:T(8,128)S(1)} collective-permute-done((f32[1032,128]{1,0:T(8,128)S(1)}, f32[1032,128]{1,0:T(8,128)S(1)}, u32[]{:S(2)}, u32[]{:S(2)}) %collective-permute-start.9) | collective-permute-done | bytes 528416 | tf_op jit(solution)/shard_map/ppermute | solution.py:25
  42.2 1.2 collective-permute-start.12
  43.4 0.1 pad_maximum_fusion.1
  43.5 0.1 pad_maximum_fusion
  43.5 3.4 %collective-permute-done.6.refs_5_ = f32[1032,128]{1,0:T(8,128)S(1)} collective-permute-done((f32[1032,128]{1,0:T(8,128)S(1)}, f32[1032,128]{1,0:T(8,128)S(1)}, u32[]{:S(2)}, u32[]{:S(2)}) %collective-permute-start.6) | collective-permute-done | bytes 528416 | tf_op jit(solution)/shard_map/ppermute | solution.py:25
  46.9 1.2 collective-permute-done.7.refs_6_
  48.1 1.0 collective-permute-start.10
  49.2 3.5 %collective-permute-done.12.refs_7_ = f32[1032,128]{1,0:T(8,128)S(1)} collective-permute-done((f32[1032,128]{1,0:T(8,128)S(1)}, f32[1032,128]{1,0:T(8,128)S(1)}, u32[]{:S(2)}, u32[]{:S(2)}) %collective-permute-start.12) | collective-permute-done | bytes 528416 | tf_op jit(solution)/shard_map/ppermute | solution.py:25
  52.6 1.2 collective-permute-done.13.refs_8_
  53.8 1.0 pad_maximum_fusion.2
  54.9 1.0 pad_maximum_fusion.3
  55.8 5.6 %collective-permute-done.10.refs_3_ = f32[1552,128]{1,0:T(8,128)S(1)} collective-permute-done((f32[1552,128]{1,0:T(8,128)S(1)}, f32[1552,128]{1,0:T(8,128)S(1)}, u32[]{:S(2)}, u32[]{:S(2)}) %collective-permute-start.10) | collective-permute-done | bytes 794656 | tf_op jit(solution)/shard_map/ppermute | solution.py:25
  61.4 1.0 collective-permute-done.11.refs_4_
  62.4 0.2 all-gather.2.cloned.1.call-done.d_ref
  62.6 3.8 %shard_map.48 = (bf16[4096,512]{1,0:T(8,128)(2,1)S(1)}, bf16[4096,512]{1,0:T(8,128)(2,1)S(1)}) custom-call(f32[4096,512]{1,0:T(8,128)} %all-gather.2.cloned.1.call-done.d_ref), custom_call_target="tpu_custom_call" | custom-call | flops 8388608 | bytes 16777216 | tf_op jit(solution)/shard_map/pallas_call | solution.py:111
  66.5 1.5 %collective-permute-start.14 = (f32[1552,128]{1,0:T(8,128)S(1)}, f32[1552,128]{1,0:T(8,128)S(1)}, u32[]{:S(2)}, u32[]{:S(2)}) collective-permute-start(f32[1552,128]{1,0:T(8,128)S(1)} %copy-done.24), channel_id=1, source_target_pairs={{0,1},{1,2},{2,3},{3,0},{16,19},{17,16},{18,17},{19,18},{4,5},{5,6... | collective-permute-start | bytes 2383880 | tf_op jit(solution)/shard_map/ppermute | solution.py:25
  68.0 1.5 %collective-permute-start.15 = (f32[1552,128]{1,0:T(8,128)S(1)}, f32[1552,128]{1,0:T(8,128)S(1)}, u32[]{:S(2)}, u32[]{:S(2)}) collective-permute-start(f32[1552,128]{1,0:T(8,128)S(1)} %copy-done.25), channel_id=1, source_target_pairs={{0,4},{4,8},{8,12},{12,0},{16,28},{20,16},{24,20},{28,24},{1,5},{5... | collective-permute-start | bytes 2383880 | tf_op jit(solution)/shard_map/ppermute | solution.py:25
  69.5 1.5 %collective-permute-start.16 = (f32[1552,128]{1,0:T(8,128)S(1)}, f32[1552,128]{1,0:T(8,128)S(1)}, u32[]{:S(2)}, u32[]{:S(2)}) collective-permute-start(f32[1552,128]{1,0:T(8,128)S(1)} %collective-permute-done.10.refs_3_), channel_id=1, source_target_pairs={{0,1},{1,2},{2,3},{3,0},{16,19},{17,16},{18,17},{19,18},{4,5},{5,6... | collective-permute-start | bytes 2383880 | tf_op jit(solution)/shard_map/ppermute | solution.py:25
  71.0 1.5 %collective-permute-start.17 = (f32[1552,128]{1,0:T(8,128)S(1)}, f32[1552,128]{1,0:T(8,128)S(1)}, u32[]{:S(2)}, u32[]{:S(2)}) collective-permute-start(f32[1552,128]{1,0:T(8,128)S(1)} %collective-permute-done.11.refs_4_), channel_id=1, source_target_pairs={{0,4},{4,8},{8,12},{12,0},{16,28},{20,16},{24,20},{28,24},{1,5},{5... | collective-permute-start | bytes 2383880 | tf_op jit(solution)/shard_map/ppermute | solution.py:25
  72.4 7.4 %collective-permute-done.14.refs_5_ = f32[1552,128]{1,0:T(8,128)S(1)} collective-permute-done((f32[1552,128]{1,0:T(8,128)S(1)}, f32[1552,128]{1,0:T(8,128)S(1)}, u32[]{:S(2)}, u32[]{:S(2)}) %collective-permute-start.14) | collective-permute-done | bytes 794656 | tf_op jit(solution)/shard_map/ppermute | solution.py:25
  79.8 1.5 %collective-permute-done.15.refs_6_ = f32[1552,128]{1,0:T(8,128)S(1)} collective-permute-done((f32[1552,128]{1,0:T(8,128)S(1)}, f32[1552,128]{1,0:T(8,128)S(1)}, u32[]{:S(2)}, u32[]{:S(2)}) %collective-permute-start.15) | collective-permute-done | bytes 794656 | tf_op jit(solution)/shard_map/ppermute | solution.py:25
  81.3 1.5 %collective-permute-start.18 = (f32[1552,128]{1,0:T(8,128)S(1)}, f32[1552,128]{1,0:T(8,128)S(1)}, u32[]{:S(2)}, u32[]{:S(2)}) collective-permute-start(f32[1552,128]{1,0:T(8,128)S(1)} %collective-permute-done.14.refs_5_), channel_id=1, source_target_pairs={{0,1},{1,2},{2,3},{3,0},{16,19},{17,16},{18,17},{19,18},{4,5},{5,6... | collective-permute-start | bytes 2383880 | tf_op jit(solution)/shard_map/ppermute | solution.py:25
  82.8 0.3 collective-permute-start.19
  83.1 5.9 %shard_map.49.refs_0_ = f32[2048,512]{1,0:T(8,128)S(1)} custom-call(bf16[4096,512]{1,0:T(8,128)(2,1)S(1)} %get-tuple-element.81.refs_0_.refs_1_, bf16[4096,512]{1,0:T(8,128)(2,1)S(1)} %get-tuple-element.82.refs_1_.refs_2_, f32[1032,128]{1,0:T(8,128)S(1)} %copy-done.17, f32[1032,128]{1,0:T(8,128)S(1)} %copy-done.19, ...), custom_call_target="tpu_custom_call" | custom-call | flops 6442450944 | bytes 4194304 | tf_op jit(solution)/shard_map/pallas_call | solution.py:190
  89.0 0.0 collective-permute-done.16.refs_3_
  89.0 0.8 collective-permute-done.17.refs_4_
  89.8 1.5 %collective-permute-start.20 = (f32[1552,128]{1,0:T(8,128)S(1)}, f32[1552,128]{1,0:T(8,128)S(1)}, u32[]{:S(2)}, u32[]{:S(2)}) collective-permute-start(f32[1552,128]{1,0:T(8,128)S(1)} %collective-permute-done.16.refs_3_), channel_id=1, source_target_pairs={{0,1},{1,2},{2,3},{3,0},{16,19},{17,16},{18,17},{19,18},{4,5},{5,6... | collective-permute-start | bytes 2383880 | tf_op jit(solution)/shard_map/ppermute | solution.py:25
  91.3 0.5 collective-permute-start.21
  91.8 5.0 %shard_map.50.refs_0_ = f32[2048,512]{1,0:T(8,128)S(1)} custom-call(f32[2048,512]{1,0:T(8,128)S(1)} %shard_map.49.refs_0_, bf16[4096,512]{1,0:T(8,128)(2,1)S(1)} %get-tuple-element.81.refs_0_.refs_1_, bf16[4096,512]{1,0:T(8,128)(2,1)S(1)} %get-tuple-element.82.refs_1_.refs_2_, f32[1032,128]{1,0:T(8,128)S(1)} %copy-done.7, ...), custom_call_target="tpu_custom_call", output_to_operand_aliasing={{}: (0, {})} | custom-call | flops 4831838208 | bytes 3145728 | tf_op jit(solution)/shard_map/pallas_call | solution.py:190
  96.8 0.0 collective-permute-done.18.refs_5_
  96.9 1.5 %collective-permute-done.19.refs_6_ = f32[1552,128]{1,0:T(8,128)S(1)} collective-permute-done((f32[1552,128]{1,0:T(8,128)S(1)}, f32[1552,128]{1,0:T(8,128)S(1)}, u32[]{:S(2)}, u32[]{:S(2)}) %collective-permute-start.19) | collective-permute-done | bytes 794656 | tf_op jit(solution)/shard_map/ppermute | solution.py:25
  98.3 1.5 %collective-permute-start.22 = (f32[1552,128]{1,0:T(8,128)S(1)}, f32[1552,128]{1,0:T(8,128)S(1)}, u32[]{:S(2)}, u32[]{:S(2)}) collective-permute-start(f32[1552,128]{1,0:T(8,128)S(1)} %collective-permute-done.18.refs_5_), channel_id=1, source_target_pairs={{0,1},{1,2},{2,3},{3,0},{16,19},{17,16},{18,17},{19,18},{4,5},{5,6... | collective-permute-start | bytes 2383880 | tf_op jit(solution)/shard_map/ppermute | solution.py:25
  99.8 0.3 collective-permute-start.23
  100.1 5.1 %shard_map.51.refs_0_ = f32[2048,512]{1,0:T(8,128)S(1)} custom-call(f32[2048,512]{1,0:T(8,128)S(1)} %shard_map.50.refs_0_, bf16[4096,512]{1,0:T(8,128)(2,1)S(1)} %get-tuple-element.81.refs_0_.refs_1_, bf16[4096,512]{1,0:T(8,128)(2,1)S(1)} %get-tuple-element.82.refs_1_.refs_2_, ...), custom_call_target="tpu_custom_call", output_to_operand_aliasing={{}: (0, {})} | custom-call | flops 4831838208 | bytes 3145728 | tf_op jit(solution)/shard_map/pallas_call | solution.py:190
  105.2 0.2 collective-permute-done.20.refs_7_
  105.4 1.5 %collective-permute-done.21.refs_8_ = f32[1552,128]{1,0:T(8,128)S(1)} collective-permute-done((f32[1552,128]{1,0:T(8,128)S(1)}, f32[1552,128]{1,0:T(8,128)S(1)}, u32[]{:S(2)}, u32[]{:S(2)}) %collective-permute-start.21) | collective-permute-done | bytes 794656 | tf_op jit(solution)/shard_map/ppermute | solution.py:25
  106.8 7.0 %shard_map.52.refs_0_ = f32[2048,512]{1,0:T(8,128)S(1)} custom-call(f32[2048,512]{1,0:T(8,128)S(1)} %shard_map.51.refs_0_, bf16[4096,512]{1,0:T(8,128)(2,1)S(1)} %get-tuple-element.81.refs_0_.refs_1_, bf16[4096,512]{1,0:T(8,128)(2,1)S(1)} %get-tuple-element.82.refs_1_.refs_2_, ...), custom_call_target="tpu_custom_call", output_to_operand_aliasing={{}: (0, {})} | custom-call | flops 7247757312 | bytes 4718592 | tf_op jit(solution)/shard_map/pallas_call | solution.py:190
  113.9 1.5 %collective-permute-done.23.refs_4_ = f32[1552,128]{1,0:T(8,128)S(1)} collective-permute-done((f32[1552,128]{1,0:T(8,128)S(1)}, f32[1552,128]{1,0:T(8,128)S(1)}, u32[]{:S(2)}, u32[]{:S(2)}) %collective-permute-start.23) | collective-permute-done | bytes 794656 | tf_op jit(solution)/shard_map/ppermute | solution.py:25
  115.3 4.8 %shard_map.53 = f32[2048,512]{1,0:T(8,128)} custom-call(f32[2048,512]{1,0:T(8,128)S(1)} %shard_map.52.refs_0_, bf16[4096,512]{1,0:T(8,128)(2,1)S(1)} %get-tuple-element.81.refs_0_.refs_1_, bf16[4096,512]{1,0:T(8,128)(2,1)S(1)} %get-tuple-element.82.refs_1_.refs_2_, f32[1552,128]{1,0:T(8,128)S(1)} %collective-permute-done.22.refs_3_, ...), custom_call_target="tpu_custom_call" | custom-call | flops 2415919104 | bytes 1572864 | tf_op jit(solution)/shard_map/pallas_call | solution.py:190
  (62 shorter events, 0.3 us)
Async XLA Ops:
  6.5 56.1 %all-gather.2.cloned.1.call-start = ((), (), s32[]{:S(2)}) async-start(), calls=%async_computation | async-start | bytes 9437184 | tf_op jit(solution)/shard_map/all_gather | solution.py:210
  6.5 0.7 copy-start.14
  10.0 0.7 copy-start.15
  12.5 10.5 %collective-permute-start = (f32[1032,128]{1,0:T(8,128)S(1)}, f32[1032,128]{1,0:T(8,128)S(1)}, u32[]{:S(2)}, u32[]{:S(2)}) collective-permute-start(f32[1032,128]{1,0:T(8,128)S(1)} %get-tuple-element.52.refs_2_), channel_id=1, source_target_pairs={{0,1},{1,2},{2,3},{3,0},{16,19},{17,16},{18,17},{19,18},{4,5},{5,6... | collective-permute-start | bytes 1585160 | tf_op jit(solution)/shard_map/ppermute | solution.py:25
  14.1 10.4 %collective-permute-start.1 = (f32[1032,128]{1,0:T(8,128)S(1)}, f32[1032,128]{1,0:T(8,128)S(1)}, u32[]{:S(2)}, u32[]{:S(2)}) collective-permute-start(f32[1032,128]{1,0:T(8,128)S(1)} %get-tuple-element.53.refs_3_), channel_id=1, source_target_pairs={{0,4},{4,8},{8,12},{12,0},{16,28},{20,16},{24,20},{28,24},{1,5},{5... | collective-permute-start | bytes 1585160 | tf_op jit(solution)/shard_map/ppermute | solution.py:25
  15.7 14.5 %collective-permute-start.5 = (f32[1032,128]{1,0:T(8,128)S(1)}, f32[1032,128]{1,0:T(8,128)S(1)}, u32[]{:S(2)}, u32[]{:S(2)}) collective-permute-start(f32[1032,128]{1,0:T(8,128)S(1)} %get-tuple-element.52.refs_2_), channel_id=1, source_target_pairs={{0,4},{4,8},{8,12},{12,0},{16,28},{20,16},{24,20},{28,24},{1,5},{5... | collective-permute-start | bytes 1585160 | tf_op jit(solution)/shard_map/ppermute | solution.py:25
  17.3 0.8 copy-start.16
  18.1 12.1 %collective-permute-start.4 = (f32[1032,128]{1,0:T(8,128)S(1)}, f32[1032,128]{1,0:T(8,128)S(1)}, u32[]{:S(2)}, u32[]{:S(2)}) collective-permute-start(f32[1032,128]{1,0:T(8,128)S(1)} %get-tuple-element.53.refs_3_), channel_id=1, source_target_pairs={{0,1},{1,2},{2,3},{3,0},{16,19},{17,16},{18,17},{19,18},{4,5},{5,6... | collective-permute-start | bytes 1585160 | tf_op jit(solution)/shard_map/ppermute | solution.py:25
  19.6 0.8 copy-start.18
  24.5 11.9 %copy-start = (f32[1032,128]{1,0:T(8,128)}, f32[1032,128]{1,0:T(8,128)S(1)}, u32[]{:S(2)}) copy-start(f32[1032,128]{1,0:T(8,128)S(1)} %collective-permute-done.1.refs_5_) | copy-start | bytes 1585156
  24.5 10.4 %collective-permute-start.2 = (f32[1032,128]{1,0:T(8,128)S(1)}, f32[1032,128]{1,0:T(8,128)S(1)}, u32[]{:S(2)}, u32[]{:S(2)}) collective-permute-start(f32[1032,128]{1,0:T(8,128)S(1)} %collective-permute-done.refs_4_), channel_id=1, source_target_pairs={{0,1},{1,2},{2,3},{3,0},{16,19},{17,16},{18,17},{19,18},{4,5},{5,6... | collective-permute-start | bytes 1585160 | tf_op jit(solution)/shard_map/ppermute | solution.py:25
  26.0 10.4 %collective-permute-start.3 = (f32[1032,128]{1,0:T(8,128)S(1)}, f32[1032,128]{1,0:T(8,128)S(1)}, u32[]{:S(2)}, u32[]{:S(2)}) collective-permute-start(f32[1032,128]{1,0:T(8,128)S(1)} %collective-permute-done.1.refs_5_), channel_id=1, source_target_pairs={{0,4},{4,8},{8,12},{12,0},{16,28},{20,16},{24,20},{28,24},{1,5},{5... | collective-permute-start | bytes 1585160 | tf_op jit(solution)/shard_map/ppermute | solution.py:25
  30.2 10.5 %copy-start.20 = (f32[1032,128]{1,0:T(8,128)}, f32[1032,128]{1,0:T(8,128)S(1)}, u32[]{:S(2)}) copy-start(f32[1032,128]{1,0:T(8,128)S(1)} %collective-permute-done.5.refs_7_) | copy-start | bytes 1585156
  30.2 12.0 %copy-start.22 = (f32[1032,128]{1,0:T(8,128)}, f32[1032,128]{1,0:T(8,128)S(1)}, u32[]{:S(2)}) copy-start(f32[1032,128]{1,0:T(8,128)S(1)} %collective-permute-done.4.refs_6_) | copy-start | bytes 1585156
  30.2 10.5 %collective-permute-start.8 = (f32[1032,128]{1,0:T(8,128)S(1)}, f32[1032,128]{1,0:T(8,128)S(1)}, u32[]{:S(2)}, u32[]{:S(2)}) collective-permute-start(f32[1032,128]{1,0:T(8,128)S(1)} %collective-permute-done.4.refs_6_), channel_id=1, source_target_pairs={{0,1},{1,2},{2,3},{3,0},{16,19},{17,16},{18,17},{19,18},{4,5},{5,6... | collective-permute-start | bytes 1585160 | tf_op jit(solution)/shard_map/ppermute | solution.py:25
  31.8 10.4 %collective-permute-start.9 = (f32[1032,128]{1,0:T(8,128)S(1)}, f32[1032,128]{1,0:T(8,128)S(1)}, u32[]{:S(2)}, u32[]{:S(2)}) collective-permute-start(f32[1032,128]{1,0:T(8,128)S(1)} %collective-permute-done.5.refs_7_), channel_id=1, source_target_pairs={{0,4},{4,8},{8,12},{12,0},{16,28},{20,16},{24,20},{28,24},{1,5},{5... | collective-permute-start | bytes 1585160 | tf_op jit(solution)/shard_map/ppermute | solution.py:25
  35.0 11.9 %copy-start.2 = (f32[1032,128]{1,0:T(8,128)}, f32[1032,128]{1,0:T(8,128)S(1)}, u32[]{:S(2)}) copy-start(f32[1032,128]{1,0:T(8,128)S(1)} %collective-permute-done.2.refs_8_) | copy-start | bytes 1585156
  36.5 10.4 %copy-start.4 = (f32[1032,128]{1,0:T(8,128)}, f32[1032,128]{1,0:T(8,128)S(1)}, u32[]{:S(2)}) copy-start(f32[1032,128]{1,0:T(8,128)S(1)} %collective-permute-done.3.refs_9_) | copy-start | bytes 1585156
  36.5 10.4 %collective-permute-start.6 = (f32[1032,128]{1,0:T(8,128)S(1)}, f32[1032,128]{1,0:T(8,128)S(1)}, u32[]{:S(2)}, u32[]{:S(2)}) collective-permute-start(f32[1032,128]{1,0:T(8,128)S(1)} %collective-permute-done.2.refs_8_), channel_id=1, source_target_pairs={{0,1},{1,2},{2,3},{3,0},{16,19},{17,16},{18,17},{19,18},{4,5},{5,6... | collective-permute-start | bytes 1585160 | tf_op jit(solution)/shard_map/ppermute | solution.py:25
  37.7 10.4 %collective-permute-start.7 = (f32[1032,128]{1,0:T(8,128)S(1)}, f32[1032,128]{1,0:T(8,128)S(1)}, u32[]{:S(2)}, u32[]{:S(2)}) collective-permute-start(f32[1032,128]{1,0:T(8,128)S(1)} %collective-permute-done.3.refs_9_), channel_id=1, source_target_pairs={{0,4},{4,8},{8,12},{12,0},{16,28},{20,16},{24,20},{28,24},{1,5},{5... | collective-permute-start | bytes 1585160 | tf_op jit(solution)/shard_map/ppermute | solution.py:25
  40.7 15.1 %copy-start.6 = (f32[1032,128]{1,0:T(8,128)}, f32[1032,128]{1,0:T(8,128)S(1)}, u32[]{:S(2)}) copy-start(f32[1032,128]{1,0:T(8,128)S(1)} %collective-permute-done.8.refs_3_) | copy-start | bytes 1585156
  42.2 13.6 %copy-start.8 = (f32[1032,128]{1,0:T(8,128)}, f32[1032,128]{1,0:T(8,128)S(1)}, u32[]{:S(2)}) copy-start(f32[1032,128]{1,0:T(8,128)S(1)} %collective-permute-done.9.refs_4_) | copy-start | bytes 1585156
  42.2 10.4 %collective-permute-start.12 = (f32[1032,128]{1,0:T(8,128)S(1)}, f32[1032,128]{1,0:T(8,128)S(1)}, u32[]{:S(2)}, u32[]{:S(2)}) collective-permute-start(f32[1032,128]{1,0:T(8,128)S(1)} %collective-permute-done.8.refs_3_), channel_id=1, source_target_pairs={{0,1},{1,2},{2,3},{3,0},{16,19},{17,16},{18,17},{19,18},{4,5},{5,6... | collective-permute-start | bytes 1585160 | tf_op jit(solution)/shard_map/ppermute | solution.py:25
  43.4 10.4 %collective-permute-start.13 = (f32[1032,128]{1,0:T(8,128)S(1)}, f32[1032,128]{1,0:T(8,128)S(1)}, u32[]{:S(2)}, u32[]{:S(2)}) collective-permute-start(f32[1032,128]{1,0:T(8,128)S(1)} %collective-permute-done.9.refs_4_), channel_id=1, source_target_pairs={{0,4},{4,8},{8,12},{12,0},{16,28},{20,16},{24,20},{28,24},{1,5},{5... | collective-permute-start | bytes 1585160 | tf_op jit(solution)/shard_map/ppermute | solution.py:25
  48.1 13.3 %collective-permute-start.10 = (f32[1552,128]{1,0:T(8,128)S(1)}, f32[1552,128]{1,0:T(8,128)S(1)}, u32[]{:S(2)}, u32[]{:S(2)}) collective-permute-start(f32[1552,128]{1,0:T(8,128)S(1)} %pad_maximum_fusion), channel_id=1, source_target_pairs={{0,1},{1,2},{2,3},{3,0},{16,19},{17,16},{18,17},{19,18},{4,5},{5,6... | collective-permute-start | bytes 2383880 | tf_op jit(solution)/shard_map/ppermute | solution.py:25
  49.1 13.3 %collective-permute-start.11 = (f32[1552,128]{1,0:T(8,128)S(1)}, f32[1552,128]{1,0:T(8,128)S(1)}, u32[]{:S(2)}, u32[]{:S(2)}) collective-permute-start(f32[1552,128]{1,0:T(8,128)S(1)} %pad_maximum_fusion.1), channel_id=1, source_target_pairs={{0,4},{4,8},{8,12},{12,0},{16,28},{20,16},{24,20},{28,24},{1,5},{5... | collective-permute-start | bytes 2383880 | tf_op jit(solution)/shard_map/ppermute | solution.py:25
  52.6 8.8 %copy-start.10 = (f32[1032,128]{1,0:T(8,128)}, f32[1032,128]{1,0:T(8,128)S(1)}, u32[]{:S(2)}) copy-start(f32[1032,128]{1,0:T(8,128)S(1)} %collective-permute-done.12.refs_7_) | copy-start | bytes 1585156
  53.8 7.6 %copy-start.12 = (f32[1032,128]{1,0:T(8,128)}, f32[1032,128]{1,0:T(8,128)S(1)}, u32[]{:S(2)}) copy-start(f32[1032,128]{1,0:T(8,128)S(1)} %collective-permute-done.13.refs_8_) | copy-start | bytes 1585156
  62.6 3.8 %copy-start.24 = (f32[1552,128]{1,0:T(8,128)S(1)}, f32[1552,128]{1,0:T(8,128)}, u32[]{:S(2)}) copy-start(f32[1552,128]{1,0:T(8,128)} %pad_maximum_fusion.2) | copy-start | bytes 2383876
  62.6 5.4 %copy-start.25 = (f32[1552,128]{1,0:T(8,128)S(1)}, f32[1552,128]{1,0:T(8,128)}, u32[]{:S(2)}) copy-start(f32[1552,128]{1,0:T(8,128)} %pad_maximum_fusion.3) | copy-start | bytes 2383876
  62.6 20.4 %copy-start.1 = (f32[1032,128]{1,0:T(8,128)S(1)}, f32[1032,128]{1,0:T(8,128)}, u32[]{:S(2)}) copy-start(f32[1032,128]{1,0:T(8,128)} %copy-done) | copy-start | bytes 1585156
  62.6 20.4 %copy-start.3 = (f32[1032,128]{1,0:T(8,128)S(1)}, f32[1032,128]{1,0:T(8,128)}, u32[]{:S(2)}) copy-start(f32[1032,128]{1,0:T(8,128)} %copy-done.2) | copy-start | bytes 1585156
  62.6 20.4 %copy-start.5 = (f32[1032,128]{1,0:T(8,128)S(1)}, f32[1032,128]{1,0:T(8,128)}, u32[]{:S(2)}) copy-start(f32[1032,128]{1,0:T(8,128)} %copy-done.4) | copy-start | bytes 1585156
  62.6 20.4 %copy-start.17 = (f32[1032,128]{1,0:T(8,128)S(1)}, f32[1032,128]{1,0:T(8,128)}, u32[]{:S(2)}) copy-start(f32[1032,128]{1,0:T(8,128)} %copy-done.16) | copy-start | bytes 1585156
  62.6 20.4 %copy-start.19 = (f32[1032,128]{1,0:T(8,128)S(1)}, f32[1032,128]{1,0:T(8,128)}, u32[]{:S(2)}) copy-start(f32[1032,128]{1,0:T(8,128)} %copy-done.18) | copy-start | bytes 1585156
  62.6 20.4 %copy-start.21 = (f32[1032,128]{1,0:T(8,128)S(1)}, f32[1032,128]{1,0:T(8,128)}, u32[]{:S(2)}) copy-start(f32[1032,128]{1,0:T(8,128)} %copy-done.20) | copy-start | bytes 1585156
  62.6 20.4 %copy-start.23 = (f32[1032,128]{1,0:T(8,128)S(1)}, f32[1032,128]{1,0:T(8,128)}, u32[]{:S(2)}) copy-start(f32[1032,128]{1,0:T(8,128)} %copy-done.22) | copy-start | bytes 1585156
  66.4 25.4 %copy-start.7 = (f32[1032,128]{1,0:T(8,128)S(1)}, f32[1032,128]{1,0:T(8,128)}, u32[]{:S(2)}) copy-start(f32[1032,128]{1,0:T(8,128)} %copy-done.6) | copy-start | bytes 1585156
  66.4 25.4 %copy-start.9 = (f32[1032,128]{1,0:T(8,128)S(1)}, f32[1032,128]{1,0:T(8,128)}, u32[]{:S(2)}) copy-start(f32[1032,128]{1,0:T(8,128)} %copy-done.8) | copy-start | bytes 1585156
  66.4 25.3 %copy-start.11 = (f32[1032,128]{1,0:T(8,128)S(1)}, f32[1032,128]{1,0:T(8,128)}, u32[]{:S(2)}) copy-start(f32[1032,128]{1,0:T(8,128)} %copy-done.10) | copy-start | bytes 1585156
  66.5 25.3 %copy-start.13 = (f32[1032,128]{1,0:T(8,128)S(1)}, f32[1032,128]{1,0:T(8,128)}, u32[]{:S(2)}) copy-start(f32[1032,128]{1,0:T(8,128)} %copy-done.12) | copy-start | bytes 1585156
  66.5 13.4 %collective-permute-start.14 = (f32[1552,128]{1,0:T(8,128)S(1)}, f32[1552,128]{1,0:T(8,128)S(1)}, u32[]{:S(2)}, u32[]{:S(2)}) collective-permute-start(f32[1552,128]{1,0:T(8,128)S(1)} %copy-done.24), channel_id=1, source_target_pairs={{0,1},{1,2},{2,3},{3,0},{16,19},{17,16},{18,17},{19,18},{4,5},{5,6... | collective-permute-start | bytes 2383880 | tf_op jit(solution)/shard_map/ppermute | solution.py:25
  68.0 13.3 %collective-permute-start.15 = (f32[1552,128]{1,0:T(8,128)S(1)}, f32[1552,128]{1,0:T(8,128)S(1)}, u32[]{:S(2)}, u32[]{:S(2)}) collective-permute-start(f32[1552,128]{1,0:T(8,128)S(1)} %copy-done.25), channel_id=1, source_target_pairs={{0,4},{4,8},{8,12},{12,0},{16,28},{20,16},{24,20},{28,24},{1,5},{5... | collective-permute-start | bytes 2383880 | tf_op jit(solution)/shard_map/ppermute | solution.py:25
  69.5 19.5 %collective-permute-start.16 = (f32[1552,128]{1,0:T(8,128)S(1)}, f32[1552,128]{1,0:T(8,128)S(1)}, u32[]{:S(2)}, u32[]{:S(2)}) collective-permute-start(f32[1552,128]{1,0:T(8,128)S(1)} %collective-permute-done.10.refs_3_), channel_id=1, source_target_pairs={{0,1},{1,2},{2,3},{3,0},{16,19},{17,16},{18,17},{19,18},{4,5},{5,6... | collective-permute-start | bytes 2383880 | tf_op jit(solution)/shard_map/ppermute | solution.py:25
  71.0 18.8 %collective-permute-start.17 = (f32[1552,128]{1,0:T(8,128)S(1)}, f32[1552,128]{1,0:T(8,128)S(1)}, u32[]{:S(2)}, u32[]{:S(2)}) collective-permute-start(f32[1552,128]{1,0:T(8,128)S(1)} %collective-permute-done.11.refs_4_), channel_id=1, source_target_pairs={{0,4},{4,8},{8,12},{12,0},{16,28},{20,16},{24,20},{28,24},{1,5},{5... | collective-permute-start | bytes 2383880 | tf_op jit(solution)/shard_map/ppermute | solution.py:25
  81.3 15.6 %collective-permute-start.18 = (f32[1552,128]{1,0:T(8,128)S(1)}, f32[1552,128]{1,0:T(8,128)S(1)}, u32[]{:S(2)}, u32[]{:S(2)}) collective-permute-start(f32[1552,128]{1,0:T(8,128)S(1)} %collective-permute-done.14.refs_5_), channel_id=1, source_target_pairs={{0,1},{1,2},{2,3},{3,0},{16,19},{17,16},{18,17},{19,18},{4,5},{5,6... | collective-permute-start | bytes 2383880 | tf_op jit(solution)/shard_map/ppermute | solution.py:25
  82.8 15.6 %collective-permute-start.19 = (f32[1552,128]{1,0:T(8,128)S(1)}, f32[1552,128]{1,0:T(8,128)S(1)}, u32[]{:S(2)}, u32[]{:S(2)}) collective-permute-start(f32[1552,128]{1,0:T(8,128)S(1)} %collective-permute-done.15.refs_6_), channel_id=1, source_target_pairs={{0,4},{4,8},{8,12},{12,0},{16,28},{20,16},{24,20},{28,24},{1,5},{5... | collective-permute-start | bytes 2383880 | tf_op jit(solution)/shard_map/ppermute | solution.py:25
  89.8 15.6 %collective-permute-start.20 = (f32[1552,128]{1,0:T(8,128)S(1)}, f32[1552,128]{1,0:T(8,128)S(1)}, u32[]{:S(2)}, u32[]{:S(2)}) collective-permute-start(f32[1552,128]{1,0:T(8,128)S(1)} %collective-permute-done.16.refs_3_), channel_id=1, source_target_pairs={{0,1},{1,2},{2,3},{3,0},{16,19},{17,16},{18,17},{19,18},{4,5},{5,6... | collective-permute-start | bytes 2383880 | tf_op jit(solution)/shard_map/ppermute | solution.py:25
  91.3 15.6 %collective-permute-start.21 = (f32[1552,128]{1,0:T(8,128)S(1)}, f32[1552,128]{1,0:T(8,128)S(1)}, u32[]{:S(2)}, u32[]{:S(2)}) collective-permute-start(f32[1552,128]{1,0:T(8,128)S(1)} %collective-permute-done.17.refs_4_), channel_id=1, source_target_pairs={{0,4},{4,8},{8,12},{12,0},{16,28},{20,16},{24,20},{28,24},{1,5},{5... | collective-permute-start | bytes 2383880 | tf_op jit(solution)/shard_map/ppermute | solution.py:25
  98.3 15.6 %collective-permute-start.22 = (f32[1552,128]{1,0:T(8,128)S(1)}, f32[1552,128]{1,0:T(8,128)S(1)}, u32[]{:S(2)}, u32[]{:S(2)}) collective-permute-start(f32[1552,128]{1,0:T(8,128)S(1)} %collective-permute-done.18.refs_5_), channel_id=1, source_target_pairs={{0,1},{1,2},{2,3},{3,0},{16,19},{17,16},{18,17},{19,18},{4,5},{5,6... | collective-permute-start | bytes 2383880 | tf_op jit(solution)/shard_map/ppermute | solution.py:25
  99.8 15.6 %collective-permute-start.23 = (f32[1552,128]{1,0:T(8,128)S(1)}, f32[1552,128]{1,0:T(8,128)S(1)}, u32[]{:S(2)}, u32[]{:S(2)}) collective-permute-start(f32[1552,128]{1,0:T(8,128)S(1)} %collective-permute-done.19.refs_6_), channel_id=1, source_target_pairs={{0,4},{4,8},{8,12},{12,0},{16,28},{20,16},{24,20},{28,24},{1,5},{5... | collective-permute-start | bytes 2383880 | tf_op jit(solution)/shard_map/ppermute | solution.py:25
Sparse Core Ops, SparseCore 0:
  10.2 52.3 all-gather.1
